TPU v7x, 512 devices: a whole 4x4x16 slice. The times are simulated.
512 devices in a mesh: scan: 64 (over y_lo, z, core), tile: 8 (over y_hi, x).
Axes of the slice: x: 4, y: 4 (y_hi: 2, y_lo: 2; y = y_hi * 2 + y_lo), z: 16, core: 2. Of those that a mesh axis runs over, the one named last changes fastest.
Arguments:
- specimen: float32 [2, 2, 1024, 512], P(None, None, 'tile'), may hold values from -6 to 6
- probe_modes: float32 [4, 2, 128, 128], P(None, None, 'tile'), may hold values from -6 to 6
- offsets: int32 [2, 512], P(None, 'scan'), may hold values from 0 to 896, as said below
- intensity: float32 [512, 128, 128], P('scan'), may hold values from 0.2 to 4
Outputs:
- specimen_grad: float32 [2, 2, 1024, 512], P(None, None, 'tile')
- probe_grad: float32 [4, 2, 128, 128], P(None, None, 'tile')
Inputs may be any that keep to these rules, and one draw needn't show every extreme that they name: Let a strip be a run of 128 rows starting at a multiple of 128. Among the 8 positions of one aligned block of the batch (the positions held by one index of scan), at most 2 have their row offset in one strip, and some strip holds exactly 2 in every block. A row offset in the last strip equals 896. Column offsets lie in 0 .. 384.
All inputs are finite; a program needn't handle non-finite values.
Results may differ from a plain program's by a relative error of at most 0.0003.
Values sent between devices are 32-bit elements; how exact they have to be, the bound alone decides.
A program may use at most 64 MiB of HBM per device.

v0:
```python
from functools import partial
import math

import jax
import jax.numpy as jnp
from jax import lax
from jax.sharding import PartitionSpec as P

fresnel_phase = 40.0
contract = partial(jnp.einsum, precision=lax.Precision.HIGHEST)


def from_behind(value, axis, steps):
    count = lax.axis_size(axis)
    initial, last = (max(0, -steps), min(count, count - steps))
    return lax.ppermute(value, axis, [(source, source + steps) for source in range(initial, last)])


def dft_tables(extent):
    counter = jnp.arange(extent, dtype=jnp.int32)
    product = counter[:, None] * counter[None, :] % extent
    angle = product.astype(jnp.float32) * (-2.0 * math.pi / extent)
    norm_factor = 1.0 / math.sqrt(extent)
    frequency = ((counter + extent // 2) % extent - extent // 2).astype(jnp.float32) / extent
    phase_map = -fresnel_phase * (frequency[:, None] ** 2 + frequency[None, :] ** 2)
    return (
        jnp.cos(angle) * norm_factor,
        jnp.sin(angle) * norm_factor,
        jnp.cos(phase_map),
        jnp.sin(phase_map),
    )


def left_apply(table_re, table_im, real_part, imag_part):
    out_re = contract("jk,...kl->...jl", table_re, real_part) - contract(
        "jk,...kl->...jl", table_im, imag_part
    )
    out_im = contract("jk,...kl->...jl", table_re, imag_part) + contract(
        "jk,...kl->...jl", table_im, real_part
    )
    return (out_re, out_im)


def right_apply(real_part, imag_part, table_re, table_im):
    out_re = contract("...jk,kl->...jl", real_part, table_re) - contract(
        "...jk,kl->...jl", imag_part, table_im
    )
    out_im = contract("...jk,kl->...jl", imag_part, table_re) + contract(
        "...jk,kl->...jl", real_part, table_im
    )
    return (out_re, out_im)


def transform(real_part, imag_part, table_re, table_im):
    middle_re, middle_im = left_apply(table_re, table_im, real_part, imag_part)
    return right_apply(middle_re, middle_im, table_re, table_im)


def slot_loss(patch_set, probe_set, measured, weights, tables):
    table_re, table_im, kernel_re, kernel_im = tables
    wave_re = probe_set[:, 0][None]
    wave_im = probe_set[:, 1][None]
    for depth in range(patch_set.shape[1]):
        layer_re = patch_set[:, depth, 0][:, None]
        layer_im = patch_set[:, depth, 1][:, None]
        wave_re, wave_im = (
            wave_re * layer_re - wave_im * layer_im,
            wave_re * layer_im + wave_im * layer_re,
        )
        if depth + 1 < patch_set.shape[1]:
            spec_re, spec_im = transform(wave_re, wave_im, table_re, table_im)
            spec_re, spec_im = (
                spec_re * kernel_re - spec_im * kernel_im,
                spec_re * kernel_im + spec_im * kernel_re,
            )
            wave_re, wave_im = transform(spec_re, spec_im, table_re, -table_im)
    far_re, far_im = transform(wave_re, wave_im, table_re, table_im)
    model_int = jnp.sum(far_re * far_re + far_im * far_im, axis=1)
    misfit = model_int - measured
    return 0.5 * jnp.sum(weights[:, None, None] * misfit * misfit)


def shards(specimen, probe_modes, offsets, intensity):
    tiles = lax.axis_size("tile")
    owner_index = lax.axis_index("tile")
    height = specimen.shape[2]
    extent = probe_modes.shape[3]
    per_group = offsets.shape[1]
    capacity = 2 * (per_group // tiles)
    rows_all = offsets[0]
    cols_all = offsets[1]
    owned = rows_all // height == owner_index
    slot_rank = jnp.cumsum(owned.astype(jnp.int32)) - 1
    slot_ids = jnp.arange(capacity, dtype=jnp.int32)
    selector = ((slot_rank[None, :] == slot_ids[:, None]) & owned[None, :]).astype(jnp.int32)
    filled = jnp.sum(selector, axis=1)
    local_rows = jnp.sum(selector * rows_all[None, :], axis=1) - filled * owner_index * height
    local_cols = jnp.sum(selector * cols_all[None, :], axis=1)
    weights = filled.astype(jnp.float32)
    measured = contract("cb,bij->cij", selector.astype(jnp.float32), intensity)
    below = from_behind(specimen, "tile", -1)
    extended = jnp.concatenate([specimen, below], axis=2)
    anchor = jnp.zeros((), jnp.int32)
    window = (specimen.shape[0], 2, extent, extent)
    corners = [(anchor, anchor, local_rows[slot], local_cols[slot]) for slot in range(capacity)]
    patches = jnp.stack(
        [lax.dynamic_slice(extended, corners[slot], window) for slot in range(capacity)]
    )
    probe_full = lax.all_gather(probe_modes, "tile", axis=2, tiled=True)
    tables = dft_tables(extent)

    def objective(patch_set, probe_set):
        return slot_loss(patch_set, probe_set, measured, weights, tables)

    loss_value, pullback = jax.vjp(objective, patches, probe_full)
    patch_grads, probe_grads = pullback(jnp.ones((), jnp.float32))
    canvas = jnp.zeros_like(extended)
    for slot in range(capacity):
        current = lax.dynamic_slice(canvas, corners[slot], window)
        canvas = lax.dynamic_update_slice(canvas, current + patch_grads[slot], corners[slot])
    summed = lax.psum(canvas, "scan")
    lower_rim = from_behind(summed[:, :, height:], "tile", 1)
    specimen_grad = summed[:, :, :height] + lower_rim
    probe_whole = lax.psum(probe_grads, "scan")
    probe_grad = lax.psum_scatter(probe_whole, "tile", scatter_dimension=2, tiled=True)
    return (specimen_grad, probe_grad)


def solution(mesh):
    return jax.shard_map(
        shards,
        mesh=mesh,
        in_specs=(
            P(None, None, "tile", None),
            P(None, None, "tile", None),
            P(None, "scan"),
            P("scan", None, None),
        ),
        out_specs=(P(None, None, "tile", None), P(None, None, "tile", None)),
        check_vma=False,
    )
```

profile of v0, /device:TPU:24, one launch (start us, length us, event | category | flops | bytes accessed | tf_op | source)
XLA Modules:
  0.0 695.5 jit_solution(9195932791599319527)
XLA Ops:
  7.2 5.5 collective-permute-start
  17.7 45.5 %all_gather.3 = f32[4,2,128,128]{3,2,1,0:T(8,128)S(1)} all-gather(f32[4,2,16,128]{3,2,1,0:T(8,128)} %param.5), channel_id=1, replica_groups=mesh['scan'=64,'tile'=8] {'tile'}, dimensions={2}, use_global_device_ids=true | all-gather | bytes 589824 | tf_op jit(solution)/shard_map/all_gather | solution.py:109
  69.3 1.3 dynamic-slice
  80.9 1.2 fusion.58
  82.1 1.6 fusion.59
  83.7 1.2 fusion.15
  86.1 1.2 fusion.14
  90.7 1.2 fusion.115
  91.9 1.2 fusion.111
  93.1 1.2 fusion.13
  94.3 1.4 fusion.12
  106.3 1.2 multiply_reduce_fusion.10
  118.0 1.4 fusion.95
  121.3 1.3 multiply_reduce_fusion.3
  124.7 3.2 dynamic_update_slice.6
  128.1 1.8 dynamic_update_slice.7
  129.9 97.9 %all-reduce.11.cloned.1.call-done = f32[4,2,128,128]{3,0,1,2:T(4,128)} async-done(((f32[4,2,128,128]{3,0,1,2:T(4,128)}), f32[4,2,128,128]{3,0,1,2:T(4,128)}) %all-reduce.11.cloned.1.call-update) | async-done | bytes 524304
  227.8 1.5 constant_dynamic-slice_fusion
  229.3 426.7 %all-reduce.13.cloned.1.call-done = (f32[2,2,256,512]{3,2,1,0:T(8,128)}, f32[4,2,16,128]{3,0,1,2:T(4,128)}) async-done(((f32[2,2,256,512]{3,2,1,0:T(8,128)}, f32[4,2,16,128]{3,0,1,2:T(4,128)}), (f32[2,2,256,512]{3,2,1,0:T(8,128)}, f32[4,2,16,128]{3,0,1,2:T(4,128)})) %all-reduce.13.cloned.1.call-update) | async-done | bytes 2162704 | tf_op jit(solution)/shard_map/psum | solution.py:121
  656.1 1.4 slice.75
  657.5 3.4 collective-permute-start.1
  660.9 1.5 copy.208
  662.4 24.7 %collective-permute-done.1 = f32[2,2,128,512]{3,2,1,0:T(8,128)S(1)} collective-permute-done((f32[2,2,128,512]{3,2,1,0:T(8,128)S(1)}, f32[2,2,128,512]{3,2,1,0:T(8,128)S(1)}, u32[]{:S(2)}, u32[]{:S(2)}) %collective-permute-start.1) | collective-permute-done | bytes 1048608 | tf_op jit(solution)/shard_map/ppermute | solution.py:16
  687.1 1.2 slice_add_fusion
  (86 shorter events, 42.5 us)
Async XLA Ops:
  7.2 64.5 %copy-start = (f32[8,128,128]{2,1,0:T(8,128)S(1)}, f32[8,128,128]{2,1,0:T(8,128)}, u32[]{:S(2)}) copy-start(f32[8,128,128]{2,1,0:T(8,128)} %param.7) | copy-start | bytes 1572868
  7.2 64.0 %copy-start.3 = (f32[2,2,128,512]{3,2,1,0:T(8,128)S(1)}, f32[2,2,128,512]{3,2,1,0:T(8,128)}, u32[]{:S(2)}) copy-start(f32[2,2,128,512]{3,2,1,0:T(8,128)} %param.4) | copy-start | bytes 3145732
  7.2 220.6 %all-reduce.11.cloned.1.call-start = ((), (), s32[]{:S(2)}) async-start(), calls=%async_computation | async-start | bytes 1048576
  7.2 65.2 %collective-permute-start = (f32[2,2,128,512]{3,2,1,0:T(8,128)}, f32[2,2,128,512]{3,2,1,0:T(8,128)S(1)}, u32[]{:S(2)}, u32[]{:S(2)}) collective-permute-start(f32[2,2,128,512]{3,2,1,0:T(8,128)} %param.4), channel_id=1, source_target_pairs={{1,0},{2,1},{3,2},{4,3},{5,4},{6,5},{7,6},{9,8},{10,9},{11,10},{12... | collective-permute-start | bytes 3145736 | tf_op jit(solution)/shard_map/ppermute | solution.py:16
  123.8 532.3 %all-reduce.13.cloned.1.call-start = ((), (), s32[]{:S(2)}) async-start(), calls=%async_computation.1 | async-start | bytes 4325376 | tf_op jit(solution)/shard_map/psum | solution.py:121
  129.9 99.4 %copy-start.1 = (f32[2,2,256,512]{3,2,1,0:T(8,128)}, f32[2,2,256,512]{3,2,1,0:T(8,128)S(1)}, u32[]{:S(2)}) copy-start(f32[2,2,256,512]{3,2,1,0:T(8,128)S(1)} %dynamic_update_slice.7) | copy-start | bytes 6291460
  656.1 31.0 %copy-start.2 = (f32[2,2,256,512]{3,2,1,0:T(8,128)S(1)}, f32[2,2,256,512]{3,2,1,0:T(8,128)}, u32[]{:S(2)}) copy-start(f32[2,2,256,512]{3,2,1,0:T(8,128)} %get-tuple-element.27) | copy-start | bytes 6291460
  657.5 29.5 %collective-permute-start.1 = (f32[2,2,128,512]{3,2,1,0:T(8,128)S(1)}, f32[2,2,128,512]{3,2,1,0:T(8,128)S(1)}, u32[]{:S(2)}, u32[]{:S(2)}) collective-permute-start(f32[2,2,128,512]{3,2,1,0:T(8,128)S(1)} %slice.75), channel_id=1, source_target_pairs={{0,1},{1,2},{2,3},{3,4},{4,5},{5,6},{6,7},{8,9},{9,10},{10,11},{11... | collective-permute-start | bytes 3145736 | tf_op jit(solution)/shard_map/ppermute | solution.py:16
Sparse Core Ops, SparseCore 0:
  123.9 103.8 all-reduce.10
  231.7 424.3 all-reduce.12
where the time goes:
time: 705 us; the launch traced here: 696 us
  waiting for transfers between devices  549 us (78%)
  matrix products  50 us (7%)
  blocking collectives  45.5 us (6%)
  between operations  23.4 us (3%)
  local copies, waits for them, and re-layouts  15.3 us (2%)
  starting transfers between devices  8.93 us (1%)
    psum x1, waiting for transfers between devices, shards(): summed = lax.psum(canvas, 'scan')  427 us
    unnamed x3, waiting for transfers between devices  97.9 us
    all_gather x1, blocking collectives, shards(): probe_full = lax.all_gather(probe_modes, 'tile', axis=2, tiled=True)  45.5 us
    ppermute x2, waiting for transfers between devices, from_behind(): lax.ppermute(value, axis, [(source, source + steps) for source in range(i...  24.7 us
  transfers between devices with their start and end apart: 4, of which 3 were waited for; matrix products, arithmetic and copies ran while one was open for 2% of the time, Pallas kernels for 0%

commit v1 on v0

v1 whole, which is shorter than its diff:
```python
from functools import partial
import math

import jax
import jax.numpy as jnp
import numpy as np
from jax import lax
from jax.experimental import pallas as pl
from jax.experimental.pallas import tpu as pltpu
from jax.sharding import PartitionSpec as P

fresnel_phase = 40.0
F32 = jnp.float32
BF16 = jnp.bfloat16
MESH = pl.DeviceIdType.MESH
VMEM_LIMIT = 56 * 1024 * 1024
CAP = 2


def split_bf16(table):
    high = table.astype(BF16)
    low = (table - high.astype(np.float64)).astype(BF16)
    return np.asarray(high), np.asarray(low)


def dft_tables(n):
    k = np.arange(n)
    angle = (np.outer(k, k) % n) * (-2.0 * np.pi / n)
    re, im = np.cos(angle) / math.sqrt(n), np.sin(angle) / math.sqrt(n)
    forward = np.block([[re, im], [-im, re]])
    inverse = np.block([[re, -im], [im, re]])
    fh, fl = split_bf16(forward)
    ih, il = split_bf16(inverse)
    right = np.stack([np.concatenate([fh, fh, fl], 0), np.concatenate([ih, ih, il], 0)])
    left = np.stack([np.concatenate([ih, ih, il], 1), np.concatenate([fh, fh, fl], 1)])
    freq = np.fft.fftfreq(n)
    phi = -fresnel_phase * (freq[:, None] ** 2 + freq[None, :] ** 2)
    kernel = np.stack([np.cos(phi), np.sin(phi)]).astype(np.float32)
    return right, left, kernel


class Place:
    def __init__(self, ns, nt):
        self.ns, self.nt, self.nz = ns, nt, ns // 4
        s, t = lax.axis_index("scan"), lax.axis_index("tile")
        self.s, self.t = s, t
        self.core = lax.rem(s, 2)
        self.z = lax.rem(s // 2, self.nz)
        self.ylo = s // (2 * self.nz)
        self.s_core = s + 1 - 2 * self.core
        self.s_y = lax.rem(s + ns // 2, ns)

    def s_at_z(self, z):
        return (self.ylo * self.nz + lax.rem(z + self.nz, self.nz)) * 2 + self.core

    def tile_at(self, d):
        return lax.rem(self.t + d + self.nt, self.nt)


def remote(src, dst, send, recv, s, t):
    return pltpu.make_async_remote_copy(
        src_ref=src, dst_ref=dst, send_sem=send, recv_sem=recv,
        device_id={"scan": s, "tile": t}, device_id_type=MESH,
    )


def greet(peers):
    barrier = pltpu.get_barrier_semaphore()
    for s, t in peers:
        pl.semaphore_signal(barrier, inc=1, device_id={"scan": s, "tile": t}, device_id_type=MESH)
    pl.semaphore_wait(barrier, len(peers))


PARTS = 4


def gather_stage(at, nt, spec_ref, probe_ref, ext_ref, full_ref, sems, meanwhile):
    loc_sem, xs, xr, ps, pr, zs, zr, qs, qr, cs, cr = sems
    height = spec_ref.shape[1]
    prow, n = probe_ref.shape[1:]
    step = height // PARTS
    c, z = at.core, at.z
    part = lax.rem(z, PARTS)
    steps = [1, -1, 2, -2]
    groups = [c, 2 + c]
    first, last = at.t == 0, at.t == nt - 1

    def lower(g, lo, size):
        return ext_ref.at[groups[g], pl.ds(pl.multiple_of(height + part * step + lo, 8), size), :]

    def source(g):
        return spec_ref.at[groups[g], pl.ds(pl.multiple_of(part * step, 8), step), :]

    strips = [remote(source(g), lower(g, 0, step), xs.at[g], xr.at[g], at.s, at.tile_at(-1)) for g in range(2)]
    fillers = [pltpu.make_async_copy(source(g), lower(g, 0, step), loc_sem.at[1 + g]) for g in range(2)]
    plane = 4 * c + part
    mine = pl.ds(pl.multiple_of(at.t * prow, prow), prow)
    probes = [
        remote(probe_ref.at[plane], full_ref.at[plane, mine, :], ps.at[d], pr.at[d], at.s, at.tile_at(d))
        for d in range(1, nt)
    ]
    own_probe = pltpu.make_async_copy(probe_ref.at[plane], full_ref.at[plane, mine, :], loc_sem.at[0])

    def send(g):
        pl.when(jnp.logical_not(first))(strips[g].start)
        pl.when(last)(fillers[g].start)

    def arrived(g):
        pl.when(jnp.logical_not(last))(strips[g].wait_recv)
        pl.when(last)(fillers[g].wait)

    send(0)
    for copy in probes:
        copy.start()
    own_probe.start()
    send(1)
    meanwhile()

    half = n // 2
    cuts = [(0, step), (0, step), (0, step // 2), (step // 2, step // 2)]
    spans = [pl.ds(0, n), pl.ds(0, n), pl.ds(0, half), pl.ds(half, half)]
    strip_z = [
        [
            remote(lower(g, *cuts[k]), lower(g, *cuts[k]), zs.at[g, k], zr.at[g, k], at.s_at_z(z + steps[k]), at.t)
            for k in range(4)
        ]
        for g in range(2)
    ]
    probe_z = [
        remote(full_ref.at[plane, spans[k], :], full_ref.at[plane, spans[k], :], qs.at[k], qr.at[k],
               at.s_at_z(z + steps[k]), at.t)
        for k in range(4)
    ]
    whole = [ext_ref.at[groups[g], pl.ds(height, height), :] for g in range(2)]
    whole += [full_ref.at[pl.ds(4 * c, 4)]]
    shares = [remote(whole[k], whole[k], cs.at[k], cr.at[k], at.s_core, at.t) for k in range(3)]

    arrived(0)
    for copy in strip_z[0]:
        copy.start()
    own_probe.wait()
    for copy in probes:
        copy.wait_recv()
    for copy in probe_z:
        copy.start()
    for copy in strip_z[0]:
        copy.wait_recv()
    shares[0].start()
    arrived(1)
    for copy in strip_z[1]:
        copy.start()
    for copy in probe_z:
        copy.wait_recv()
    shares[2].start()
    shares[0].wait_recv()
    shares[2].wait_recv()

    def share_later():
        for copy in strip_z[1]:
            copy.wait_recv()
        shares[1].start()

    def finish():
        shares[1].wait_recv()
        for strip in strips:
            pl.when(jnp.logical_not(first))(strip.wait_send)
        for copy in probes + strip_z[0] + strip_z[1] + probe_z + shares:
            copy.wait_send()

    return share_later, finish


def put_right(ref, m, n, part, value):
    high = value.astype(BF16)
    low = (value - high.astype(F32)).astype(BF16)
    rows = pl.ds(m * n, n)
    ref[rows, pl.ds(part * n, n)] = high
    ref[rows, pl.ds((2 + part) * n, n)] = low
    ref[rows, pl.ds((4 + part) * n, n)] = high


def put_left(ref, m, n, part, value):
    high = value.astype(BF16)
    low = (value - high.astype(F32)).astype(BF16)
    cols = pl.ds(m * n, n)
    ref[pl.ds(part * n, n), cols] = high
    ref[pl.ds((2 + part) * n, n), cols] = low
    ref[pl.ds((4 + part) * n, n), cols] = high


def split_rows(source, parts, first, rows, planes):
    for p in planes:
        value = source[p]
        high = value.astype(BF16)
        parts[2 * p, pl.ds(first, rows)] = high
        parts[2 * p + 1, pl.ds(first, rows)] = (value - high.astype(F32)).astype(BF16)


def select(condition):
    return jnp.where(condition, 1.0, 0.0).astype(BF16)


def window_stage(owner, off_ref, ext_ref, probe_ref, meas_ref, right_ref, left_ref, kern_ref,
                 canvas_ref, pgrad_ref, xa, xb, ya, yb, patch, wave, parts, cut, got, grads, tall, spread,
                 share_later, finish):
    planes, height2, width = ext_ref.shape
    height = height2 // 2
    n = probe_ref.shape[1]
    modes = probe_ref.shape[0] // 2
    per_group = off_ref.shape[1]
    batch = [(slot, m) for slot in range(CAP) for m in range(modes)]

    def dot(a, b):
        return jnp.dot(a, b, preferred_element_type=F32)

    def mul_right(src, inverse):
        return dot(src[...], right_ref[inverse])

    def mul_left(src, inverse):
        return dot(left_ref[inverse], src[...])

    def right_parts(out, b):
        rows = out[b * n:(b + 1) * n]
        return rows[:, :n], rows[:, n:]

    def left_parts(out, b):
        cols = out[:, b * n:(b + 1) * n]
        return cols[:n], cols[n:]

    def right_to_left(src, dst, inverse):
        out = mul_right(src, inverse)
        for b in range(len(batch)):
            re, im = right_parts(out, b)
            put_left(dst, b, n, 0, re)
            put_left(dst, b, n, 1, im)

    def left_to_right(src, dst, inverse):
        out = mul_left(src, inverse)
        for b in range(len(batch)):
            re, im = left_parts(out, b)
            put_right(dst, b, n, 0, re)
            put_right(dst, b, n, 1, im)

    def through_kernel(src, dst, sign):
        out = mul_left(src, 0)
        kre, kim = kern_ref[0], kern_ref[1] * sign
        for b in range(len(batch)):
            re, im = left_parts(out, b)
            put_left(dst, b, n, 0, re * kre - im * kim)
            put_left(dst, b, n, 1, re * kim + im * kre)

    hits, corners = [], []
    for slot in range(CAP):
        rank = jnp.int32(0)
        row = jnp.int32(4 * height2)
        col = jnp.int32(0)
        chosen = []
        for b in range(per_group):
            here = ((off_ref[0, b] // height) == owner).astype(jnp.int32)
            hit = here * (rank == slot).astype(jnp.int32)
            row = row + hit * (off_ref[0, b] - owner * height - 4 * height2)
            col = col + hit * off_ref[1, b]
            chosen.append(hit.astype(F32))
            rank = rank + here
        hits.append(chosen)
        corners.append((row, col))

    def iotas(*shape):
        return [lax.broadcasted_iota(jnp.int32, shape, axis) for axis in range(2)]

    i, j = iotas(width, n)
    for slot, (row, col) in enumerate(corners):
        cut[:, pl.ds(slot * n, n)] = select(i == j + col)

    def cut_windows(k):
        split_rows(ext_ref.at[:, pl.ds(height, height), :], parts, height, height, (2 * k, 2 * k + 1))
        out = dot(parts[pl.ds(4 * k, 4)].reshape(4 * height2, width), cut[...])
        for q in range(2):
            for part in range(2):
                rows = out[(2 * q + part) * height2:(2 * q + part + 1) * height2]
                for slot in range(CAP):
                    lanes = pl.ds((2 * k + q) * n, n)
                    got[slot, pl.ds(part * height2, height2), lanes] = rows[:, slot * n:(slot + 1) * n].astype(BF16)
        i, j = iotas(n, height2)
        for slot, (row, _) in enumerate(corners):
            pick = select(j == i + row)
            out = dot(jnp.concatenate([pick, pick], 1), got[slot, :, pl.ds(2 * k * n, 2 * n)])
            for q in range(2):
                patch[slot, 2 * k + q] = out[:, q * n:(q + 1) * n]

    cut_windows(0)
    for b, (slot, m) in enumerate(batch):
        pre, pim = probe_ref[2 * m], probe_ref[2 * m + 1]
        put_right(xa, b, n, 0, pre * patch[slot, 0] - pim * patch[slot, 1])
        put_right(xa, b, n, 1, pre * patch[slot, 1] + pim * patch[slot, 0])
    right_to_left(xa, ya, 0)
    through_kernel(ya, yb, 1.0)
    share_later()
    left_to_right(yb, xb, 1)
    finish()
    cut_windows(1)
    out = mul_right(xb, 1)
    for b, (slot, m) in enumerate(batch):
        re, im = right_parts(out, b)
        wave[b, 0] = re
        wave[b, 1] = im
        put_right(xa, b, n, 0, re * patch[slot, 2] - im * patch[slot, 3])
        put_right(xa, b, n, 1, re * patch[slot, 3] + im * patch[slot, 2])
    right_to_left(xa, ya, 0)
    out = mul_left(ya, 0)
    for slot in range(CAP):
        weight = sum(hits[slot])
        measured = hits[slot][0] * meas_ref[0]
        for b in range(1, per_group):
            measured = measured + hits[slot][b] * meas_ref[b]
        model = jnp.zeros((n, n), F32)
        for m in range(modes):
            re, im = left_parts(out, slot * modes + m)
            model = model + re * re + im * im
        twice = (2.0 * weight) * (model - measured)
        for m in range(modes):
            b = slot * modes + m
            re, im = left_parts(out, b)
            put_left(yb, b, n, 0, twice * re)
            put_left(yb, b, n, 1, twice * im)
    left_to_right(yb, xb, 1)
    out = mul_right(xb, 1)

    def pad_window(slot, p, grad):
        high = grad.astype(BF16)
        grads[slot, :, pl.ds(2 * p * n, n)] = high
        grads[slot, :, pl.ds((2 * p + 1) * n, n)] = (grad - high.astype(F32)).astype(BF16)

    for slot in range(CAP):
        gre = jnp.zeros((n, n), F32)
        gim = jnp.zeros((n, n), F32)
        for m in range(modes):
            b = slot * modes + m
            re, im = right_parts(out, b)
            wre, wim = wave[b, 0], wave[b, 1]
            gre = gre + wre * re + wim * im
            gim = gim + wre * im - wim * re
            put_right(xa, b, n, 0, patch[slot, 2] * re + patch[slot, 3] * im)
            put_right(xa, b, n, 1, patch[slot, 2] * im - patch[slot, 3] * re)
        pad_window(slot, 2, gre)
        pad_window(slot, 3, gim)
    right_to_left(xa, ya, 0)
    through_kernel(ya, yb, -1.0)
    left_to_right(yb, xb, 1)
    out = mul_right(xb, 1)
    for m in range(modes):
        pgre = jnp.zeros((n, n), F32)
        pgim = jnp.zeros((n, n), F32)
        for slot in range(CAP):
            re, im = right_parts(out, slot * modes + m)
            pgre = pgre + patch[slot, 0] * re + patch[slot, 1] * im
            pgim = pgim + patch[slot, 0] * im - patch[slot, 1] * re
        pgrad_ref[m, 0] = pgre
        pgrad_ref[m, 1] = pgim
    for slot in range(CAP):
        hre = jnp.zeros((n, n), F32)
        him = jnp.zeros((n, n), F32)
        for m in range(modes):
            re, im = right_parts(out, slot * modes + m)
            pre, pim = probe_ref[2 * m], probe_ref[2 * m + 1]
            hre = hre + pre * re + pim * im
            him = him + pre * im - pim * re
        pad_window(slot, 0, hre)
        pad_window(slot, 1, him)

    i, j = iotas(height2, n)
    u, v = iotas(n, width)
    for slot, (row, col) in enumerate(corners):
        out = dot(select(i == j + row), grads[slot])
        for p in range(planes):
            for part in range(2):
                piece = out[:, (2 * p + part) * n:(2 * p + part + 1) * n]
                tall[pl.ds(p * height2, height2), pl.ds((2 * slot + part) * n, n)] = piece.astype(BF16)
        put = select(v == u + col)
        spread[pl.ds(2 * slot * n, n), :] = put
        spread[pl.ds((2 * slot + 1) * n, n), :] = put
    canvas_ref[...] = dot(tall[...], spread[...]).reshape(canvas_ref.shape)


STREAMS = tuple((k, 1) for k in range(5))


OWN = 7


def sum_stage(at, nt, canvas, pgrad, gbuf, bufs, sems):
    got_c, got_p, pacc, first, upbuf, dnbuf, mine, pmine, ybuf, rimbuf, tbuf = bufs
    cs, cr, us, ur, ds_, dr, ms, mr, ts, tr, gs, gr, ks, kr = sems
    nz = at.nz
    half = nz // 2
    core, z = at.core, at.z
    own2 = pl.ds(2 * core, 2)
    other2 = pl.ds(2 - 2 * core, 2)
    lanes = 128
    def chunk(i):
        return lax.rem(i + 2 * nz, nz)

    order = [half]
    for k in range(half - 1, 0, -1):
        order += [-k, k]
    order += [0]

    def swap_at(k):
        i = order.index(k)
        return remote(canvas.at[other2, :, chunk(z + k)], got_c.at[:, :, chunk(z + k)], cs.at[i], cr.at[i], at.s_core, at.t)

    swap_p = remote(pgrad.at[other2], got_p, cs.at[nz], cr.at[nz], at.s_core, at.t)
    swaps = [swap_at(k) for k in order]
    for copy in swaps[:2] + [swap_p] + swaps[2:]:
        copy.start()

    def probe_rows():
        swap_p.wait_recv()
        for m in range(2):
            for ri in range(2):
                whole = pgrad[2 * core + m, ri] + got_p[m, ri]
                for r in range(4):
                    j = (2 * m + ri) * 4 + r
                    for t in range(nt):
                        piece = whole[16 * t + 4 * r:16 * t + 4 * r + 4]
                        pacc[j, pl.ds(4 * (t % 2), 4), pl.ds(lanes * (t // 2), lanes)] = piece

    def local(k, idx):
        j = chunk(z + k)
        if idx == 4:
            return pacc[j]
        return canvas[2 * core + idx % 2, idx // 2, j] + got_c[idx % 2, idx // 2, j]

    def up(i, p):
        part = pl.ds(*STREAMS[p])
        src = first.at[0, part] if i == 0 else upbuf.at[i - 1, part]
        return remote(src, upbuf.at[i, part], us.at[i, p], ur.at[i, p], at.s_at_z(z + 1), at.t)

    def down(i, p):
        part = pl.ds(*STREAMS[p])
        src = first.at[1, part] if i == 0 else dnbuf.at[i - 1, part]
        return remote(src, dnbuf.at[i, part], ds_.at[i, p], dr.at[i, p], at.s_at_z(z - 1), at.t)

    count = len(STREAMS)
    for k, r, start in ((half, 0, up), (1 - half, 1, down)):
        swap_at(k).wait_recv()
        for p in range(4):
            first[r, p] = local(k, p)
            start(0, p).start()
    probe_rows()
    for k, r, start in ((half, 0, up), (1 - half, 1, down)):
        first[r, 4] = local(k, 4)
        start(0, 4).start()
    for i in range(half):
        ku, kd = half - 1 - i, 2 + i - half
        if i < half - 1:
            swap_at(ku).wait_recv()
        if i < half - 2:
            swap_at(kd).wait_recv()
        for p in range(count):
            span = range(STREAMS[p][0], STREAMS[p][0] + STREAMS[p][1])
            up(i, p).wait_recv()
            if i < half - 1:
                for idx in span:
                    upbuf[i, idx] += local(ku, idx)
                up(i + 1, p).start()
                down(i, p).wait_recv()
            if i < half - 2:
                for idx in span:
                    dnbuf[i, idx] += local(kd, idx)
                down(i + 1, p).start()
    swap_at(0).wait_recv()
    for idx in range(5):
        mine[idx] = local(0, idx) + upbuf[half - 1, idx] + dnbuf[half - 2, idx]
    for q in range(nt // 2):
        pmine[q] = mine[4, :, lanes * q:lanes * (q + 1)]

    to_y = remote(mine.at[pl.ds(0, 2)], ybuf, ms.at[0], mr.at[0], at.s_y, at.t)
    rim_a = remote(mine.at[pl.ds(2, 2)], rimbuf.at[0], ms.at[1], mr.at[1], at.s, at.tile_at(1))
    rim_b = remote(mine.at[pl.ds(2, 2)], rimbuf.at[1], ms.at[2], mr.at[2], at.s_y, at.tile_at(1))
    tiles = [
        remote(pmine.at[at.tile_at(d) // 2], tbuf.at[at.ylo, at.t], ts.at[e, d], tr.at[e, d], s, at.tile_at(d))
        for e, s in ((0, at.s), (1, at.s_y)) for d in range(e ^ 1, nt)
    ]
    rim_b.start()
    rim_a.start()
    to_y.start()
    for copy in tiles:
        copy.start()
    tbuf[at.ylo, at.t] = pmine[at.t // 2]
    to_y.wait_recv()
    rim_a.wait_recv()
    rim_b.wait_recv()
    for k in range(2):
        final = (mine[k] + ybuf[k]) + (rimbuf[0, k] + rimbuf[1, k])
        for l in range(4):
            gbuf[core, OWN, 4 * k + l] = final[:, lanes * l:lanes * (l + 1)]
    for copy in tiles:
        copy.wait_recv()
    total = tbuf[0, 0]
    for k in range(1, 2 * nt):
        total = total + tbuf[k // nt, k % nt]
    gbuf[core, OWN, 8] = jnp.where(lax.rem(at.t, 2) == 1, pltpu.roll(total, 4, 0), total)

    def pass_on(i, k, to, part=slice(0, 9)):
        new = k - to + 16 * (k - to < -OWN)
        part = pl.ds(part.start, part.stop - part.start)
        return remote(gbuf.at[core, k + OWN, part], gbuf.at[core, new + OWN, part], gs.at[i], gr.at[i], at.s_at_z(z + to), at.t)

    def share(k, lo, hi):
        part = gbuf.at[core, pl.ds(lo + OWN, hi - lo + 1)]
        return remote(part, part, ks.at[k], kr.at[k], at.s_core, at.t)

    top, low = slice(0, 4), slice(4, 9)
    far = [pass_on(0, 0, 6), pass_on(1, 0, -6)]
    near = [pass_on(2, 0, 1), pass_on(3, 0, -1), pass_on(4, 0, 2), pass_on(5, 0, -2)]
    after_near = [pass_on(6, 2, -1), pass_on(7, 2, -2), pass_on(8, -2, 1), pass_on(9, -2, 2)]
    after_far = [
        pass_on(10, 6, -1), pass_on(11, 6, 1), pass_on(12, 6, -2, top),
        pass_on(13, -6, 1), pass_on(14, -6, -1), pass_on(15, -6, 2, low),
    ]
    shares = [share(0, -2, 2), share(1, 3, 4), share(2, -4, -3), share(3, 5, 8), share(4, -7, -5)]
    for copy in far + near:
        copy.start()
    near[3].wait_recv()
    near[2].wait_recv()
    near[1].wait_recv()
    near[0].wait_recv()
    for copy in after_near:
        copy.start()
    far[0].wait_recv()
    far[1].wait_recv()
    for copy in after_far:
        copy.start()
    shares[0].start()
    for copy in after_near:
        copy.wait_recv()
    shares[1].start()
    shares[2].start()
    for copy in after_far:
        copy.wait_recv()
    shares[3].start()
    shares[4].start()
    for copy in shares:
        copy.wait_recv()

    for copy in [swap_p, to_y, rim_a, rim_b] + swaps + tiles + far + near + after_near + after_far + shares:
        copy.wait_send()
    for p in range(count):
        for i in range(half):
            up(i, p).wait_send()
        for i in range(half - 1):
            down(i, p).wait_send()


def fused_kernel(ns, nt, off, spec, probe, meas_hbm, right_hbm, left_hbm, kern_hbm, gbuf, *scratch):
    ext, full, meas, right, left, kern, canvas, pgrad, xa, xb, ya, yb, patch, wave = scratch[:14]
    selecting, bufs, sems = scratch[14:20], scratch[20:31], scratch[31:]
    loads = [
        pltpu.make_async_copy(src, dst, sems[0].at[k])
        for k, (src, dst) in enumerate([(meas_hbm, meas), (right_hbm, right), (left_hbm, left), (kern_hbm, kern)])
    ]
    for copy in loads:
        copy.start()
    at = Place(ns, nt)
    z = at.z
    greet(
        [(s, at.tile_at(d)) for s in (at.s, at.s_y) for d in range(1, nt)]
        + [(at.s_at_z(z + d), at.t) for d in (1, -1, 2, -2, 6, -6)] + [(at.s_y, at.t), (at.s_core, at.t)]
    )

    def split_own():
        split_rows(spec, selecting[0], 0, spec.shape[1], range(spec.shape[0]))

    later = gather_stage(at, nt, spec, probe, ext, full, sems[1:12], split_own)
    for copy in loads:
        copy.wait()
    window_stage(at.t, off, ext, full, meas, right, left, kern, canvas, pgrad, xa, xb, ya, yb, patch, wave, *selecting, *later)
    sum_stage(at, nt, canvas, pgrad, gbuf, bufs, sems[12:])


def place_kernel(ns, nt, gbuf, out, pout):
    z = Place(ns, nt).z
    nz = gbuf.shape[1]
    lanes = gbuf.shape[4]
    for j in range(nz):
        slot = lax.rem(j - z + OWN + nz, nz)
        for c in range(2):
            for k in range(2):
                for l in range(4):
                    out[2 * c + k, j, :, lanes * l:lanes * (l + 1)] = gbuf[c, slot, 4 * k + l]
            m, ri, r = j // 8, (j // 4) % 2, j % 4
            pout[2 * c + m, ri, pl.ds(4 * r, 4), :] = gbuf[c, slot, 8, 0:4]


def shards(ns, nt, specimen, probe_modes, offsets, intensity):
    slices, two, height, width = specimen.shape
    modes, _, prow, n = probe_modes.shape
    planes = slices * two
    nz = ns // 4
    half = nz // 2
    sub = height // nz
    count = len(STREAMS)
    right, left, kernel = dft_tables(n)
    dma = pltpu.SemaphoreType.DMA
    vmem = pl.BlockSpec(memory_space=pltpu.VMEM)
    hbm = pl.BlockSpec(memory_space=pl.ANY)

    def f32(*shape):
        return pltpu.VMEM(shape, F32)

    def pair(*shape):
        return [dma(shape), dma(shape)]

    gathered = pl.pallas_call(
        partial(fused_kernel, ns, nt),
        name="gradient_sums",
        out_shape=jax.ShapeDtypeStruct((2, nz, 9, 8, n), F32),
        in_specs=[pl.BlockSpec(memory_space=pltpu.SMEM), vmem, vmem] + [hbm] * 4,
        out_specs=vmem,
        scratch_shapes=[
            f32(planes, 2 * height, width),
            f32(modes * two, n, n),
            f32(*intensity.shape),
            pltpu.VMEM(right.shape, BF16),
            pltpu.VMEM(left.shape, BF16),
            f32(2, n, n),
            f32(planes, 2, nz, sub, width),
            f32(modes, two, n, n),
            pltpu.VMEM((CAP * modes * n, 6 * n), BF16),
            pltpu.VMEM((CAP * modes * n, 6 * n), BF16),
            pltpu.VMEM((6 * n, CAP * modes * n), BF16),
            pltpu.VMEM((6 * n, CAP * modes * n), BF16),
            f32(CAP, planes, n, n),
            f32(CAP * modes, 2, n, n),
            pltpu.VMEM((2 * planes, 2 * height, width), BF16),
            pltpu.VMEM((width, CAP * n), BF16),
            pltpu.VMEM((CAP, 4 * height, planes * n), BF16),
            pltpu.VMEM((CAP, n, 2 * planes * n), BF16),
            pltpu.VMEM((planes * 2 * height, 2 * CAP * n), BF16),
            pltpu.VMEM((2 * CAP * n, width), BF16),
            f32(2, 2, nz, sub, width),
            f32(2, two, n, n),
            f32(nz, sub, width),
            f32(2, 5, sub, width),
            f32(half, 5, sub, width),
            f32(half - 1, 5, sub, width),
            f32(5, sub, width),
            f32(nt // 2, 8, n),
            f32(2, sub, width),
            f32(2, 2, sub, width),
            f32(2, nt, 8, n),
        ]
        + [dma((4,))]
        + [dma((3,))] + pair(2) + pair(nt) + pair(2, 4) + pair(4) + pair(3)
        + pair(nz + 1) + pair(half, count) + pair(half - 1, count) + pair(3) + pair(2, nt) + pair(16) + pair(5),
        compiler_params=pltpu.CompilerParams(collective_id=0, has_side_effects=True, vmem_limit_bytes=VMEM_LIMIT),
    )(
        offsets, specimen.reshape(planes, height, width), probe_modes.reshape(modes * two, prow, n), intensity,
        jnp.asarray(right), jnp.asarray(left), jnp.asarray(kernel),
    )
    out, pout = pl.pallas_call(
        partial(place_kernel, ns, nt),
        name="place_rows",
        out_shape=(
            jax.ShapeDtypeStruct((planes, nz, sub, width), F32),
            jax.ShapeDtypeStruct((modes, two, prow, n), F32),
        ),
        in_specs=[vmem],
        out_specs=[vmem] * 2,
        compiler_params=pltpu.CompilerParams(vmem_limit_bytes=VMEM_LIMIT),
    )(gathered)
    return out.reshape(specimen.shape), pout


def solution(mesh):
    ns, nt = mesh.shape["scan"], mesh.shape["tile"]
    return jax.shard_map(
        partial(shards, ns, nt),
        mesh=mesh,
        in_specs=(
            P(None, None, "tile", None),
            P(None, None, "tile", None),
            P(None, "scan"),
            P("scan", None, None),
        ),
        out_specs=(P(None, None, "tile", None), P(None, None, "tile", None)),
        check_vma=False,
    )
```

time: 705 us -> 100 us (0.14)
  the two profiles are of different devices: /device:TPU:24 before, /device:TPU:1 now
where the time goes in v1:
time: 100 us
  Pallas kernels  99.4 us (99%)
    pallas_call x1, Pallas kernels, shards(): pl.pallas_call(partial(fused_kernel, ns, nt), name='gradient_sums', out_s...  97.1 us
    pallas_call x1, Pallas kernels, shards(): pl.pallas_call(partial(place_kernel, ns, nt), name='place_rows', out_shap...  2.32 us

profile of v1, /device:TPU:1, one launch (start us, length us, event | category | flops | bytes accessed | tf_op | source)
XLA Modules:
  0.0 100.1 jit_solution(14105151496029762755)
XLA Ops:
  0.6 97.1 %gradient_sums.1.gbuf = f32[2,16,9,8,128]{4,3,2,1,0:T(8,128)} custom-call(s32[2,8]{1,0:T(2,128)} %off.1, f32[4,128,512]{2,1,0:T(8,128)} %bitcast.3, f32[8,16,128]{2,1,0:T(8,128)} %bitcast.4, f32[8,128,128]{2,1,0:T(8,128)} %meas_hbm.1, bf16[2,768,256]{2,1,0:T(8,128)(2,1)} %constant.6.clone.right_hbm, bf16[2,256,768]{2,1,0:T(8,128)(2,1)} %constant.7.clone.left_hbm, ...), custom_call_target="tpu_custom_call" | custom-call | tf_op jit(solution)/shard_map/gradient_sums/pallas_call | solution.py:615
  97.7 2.3 %place_rows.1 = (f32[4,16,8,512]{3,2,1,0:T(8,128)}, f32[4,2,16,128]{3,2,1,0:T(8,128)}) custom-call(f32[2,16,9,8,128]{4,3,2,1,0:T(8,128)} %gradient_sums.1.gbuf), custom_call_target="tpu_custom_call" | custom-call | tf_op jit(solution)/shard_map/place_rows/pallas_call | solution.py:662

commit v2 on v1

--- a/solution.py
+++ b/solution.py
@@ -162,12 +162,14 @@
 
     def finish():
         shares[1].wait_recv()
+
+    def drain():
         for strip in strips:
             pl.when(jnp.logical_not(first))(strip.wait_send)
         for copy in probes + strip_z[0] + strip_z[1] + probe_z + shares:
             copy.wait_send()
 
-    return share_later, finish
+    return share_later, finish, drain
 
 
 def put_right(ref, m, n, part, value):
@@ -382,13 +384,14 @@
     canvas_ref[...] = dot(tall[...], spread[...]).reshape(canvas_ref.shape)
 
 
-STREAMS = tuple((k, 1) for k in range(5))
+STREAMS = ((0, 2), (2, 2), (4, 1))
+AHEAD = 2
 
 
 OWN = 7
 
 
-def sum_stage(at, nt, canvas, pgrad, gbuf, bufs, sems):
+def sum_stage(at, nt, canvas, pgrad, gbuf, bufs, sems, drain):
     got_c, got_p, pacc, first, upbuf, dnbuf, mine, pmine, ybuf, rimbuf, tbuf = bufs
     cs, cr, us, ur, ds_, dr, ms, mr, ts, tr, gs, gr, ks, kr = sems
     nz = at.nz
@@ -411,7 +414,8 @@
 
     swap_p = remote(pgrad.at[other2], got_p, cs.at[nz], cr.at[nz], at.s_core, at.t)
     swaps = [swap_at(k) for k in order]
-    for copy in swaps[:2] + [swap_p] + swaps[2:]:
+    early = 2 + 2 * AHEAD
+    for copy in swaps[:2] + [swap_p] + swaps[2:early]:
         copy.start()
 
     def probe_rows():
@@ -444,15 +448,18 @@
     count = len(STREAMS)
     for k, r, start in ((half, 0, up), (1 - half, 1, down)):
         swap_at(k).wait_recv()
-        for p in range(4):
-            first[r, p] = local(k, p)
+        for p in range(count - 1):
+            for idx in range(STREAMS[p][0], STREAMS[p][0] + STREAMS[p][1]):
+                first[r, idx] = local(k, idx)
             start(0, p).start()
     probe_rows()
     for k, r, start in ((half, 0, up), (1 - half, 1, down)):
         first[r, 4] = local(k, 4)
-        start(0, 4).start()
+        start(0, count - 1).start()
     for i in range(half):
         ku, kd = half - 1 - i, 2 + i - half
+        for copy in swaps[early + 2 * i:early + 2 * i + 2]:
+            copy.start()
         if i < half - 1:
             swap_at(ku).wait_recv()
         if i < half - 2:
@@ -522,6 +529,14 @@
     shares = [share(0, -2, 2), share(1, 3, 4), share(2, -4, -3), share(3, 5, 8), share(4, -7, -5)]
     for copy in far + near:
         copy.start()
+    drain()
+    for copy in [swap_p, to_y, rim_a, rim_b] + swaps + tiles:
+        copy.wait_send()
+    for p in range(count):
+        for i in range(half):
+            up(i, p).wait_send()
+        for i in range(half - 1):
+            down(i, p).wait_send()
     near[3].wait_recv()
     near[2].wait_recv()
     near[1].wait_recv()
@@ -544,13 +559,8 @@
     for copy in shares:
         copy.wait_recv()
 
-    for copy in [swap_p, to_y, rim_a, rim_b] + swaps + tiles + far + near + after_near + after_far + shares:
+    for copy in far + near + after_near + after_far + shares:
         copy.wait_send()
-    for p in range(count):
-        for i in range(half):
-            up(i, p).wait_send()
-        for i in range(half - 1):
-            down(i, p).wait_send()
 
 
 def fused_kernel(ns, nt, off, spec, probe, meas_hbm, right_hbm, left_hbm, kern_hbm, gbuf, *scratch):
@@ -572,11 +582,12 @@
     def split_own():
         split_rows(spec, selecting[0], 0, spec.shape[1], range(spec.shape[0]))
 
-    later = gather_stage(at, nt, spec, probe, ext, full, sems[1:12], split_own)
+    share_later, finish, drain = gather_stage(at, nt, spec, probe, ext, full, sems[1:12], split_own)
     for copy in loads:
         copy.wait()
-    window_stage(at.t, off, ext, full, meas, right, left, kern, canvas, pgrad, xa, xb, ya, yb, patch, wave, *selecting, *later)
-    sum_stage(at, nt, canvas, pgrad, gbuf, bufs, sems[12:])
+    window_stage(at.t, off, ext, full, meas, right, left, kern, canvas, pgrad, xa, xb, ya, yb, patch, wave, *selecting,
+                 share_later, finish)
+    sum_stage(at, nt, canvas, pgrad, gbuf, bufs, sems[12:], drain)
 
 
 def place_kernel(ns, nt, gbuf, out, pout):

time: 100 us -> 100 us (level)
  no operation moved by 1% of the time
where the time goes in v2:
time: 100 us
  Pallas kernels  99.4 us (99%)
    pallas_call x1, Pallas kernels, shards(): pl.pallas_call(partial(fused_kernel, ns, nt), name='gradient_sums', out_s...  97.1 us
    pallas_call x1, Pallas kernels, shards(): pl.pallas_call(partial(place_kernel, ns, nt), name='place_rows', out_shap...  2.32 us

profile of v2, /device:TPU:1, one launch (start us, length us, event | category | flops | bytes accessed | tf_op | source)
XLA Modules:
  0.0 100.1 jit_solution(10435422374327824596)
XLA Ops:
  0.6 97.1 %gradient_sums.1.gbuf = f32[2,16,9,8,128]{4,3,2,1,0:T(8,128)} custom-call(s32[2,8]{1,0:T(2,128)} %off.1, f32[4,128,512]{2,1,0:T(8,128)} %bitcast.3, f32[8,16,128]{2,1,0:T(8,128)} %bitcast.4, f32[8,128,128]{2,1,0:T(8,128)} %meas_hbm.1, bf16[2,768,256]{2,1,0:T(8,128)(2,1)} %constant.6.clone.right_hbm, bf16[2,256,768]{2,1,0:T(8,128)(2,1)} %constant.7.clone.left_hbm, ...), custom_call_target="tpu_custom_call" | custom-call | tf_op jit(solution)/shard_map/gradient_sums/pallas_call | solution.py:626
  97.8 2.3 %place_rows.1 = (f32[4,16,8,512]{3,2,1,0:T(8,128)}, f32[4,2,16,128]{3,2,1,0:T(8,128)}) custom-call(f32[2,16,9,8,128]{4,3,2,1,0:T(8,128)} %gradient_sums.1.gbuf), custom_call_target="tpu_custom_call" | custom-call | tf_op jit(solution)/shard_map/place_rows/pallas_call | solution.py:673

commit v3 on v2

--- a/solution.py
+++ b/solution.py
@@ -75,7 +75,7 @@
 
 
 def gather_stage(at, nt, spec_ref, probe_ref, ext_ref, full_ref, sems, meanwhile):
-    loc_sem, xs, xr, ps, pr, zs, zr, qs, qr, cs, cr = sems
+    loc_sem, xs, xr, ps, pr, zs, zr, cs, cr = sems
     height = spec_ref.shape[1]
     prow, n = probe_ref.shape[1:]
     step = height // PARTS
@@ -93,13 +93,13 @@
 
     strips = [remote(source(g), lower(g, 0, step), xs.at[g], xr.at[g], at.s, at.tile_at(-1)) for g in range(2)]
     fillers = [pltpu.make_async_copy(source(g), lower(g, 0, step), loc_sem.at[1 + g]) for g in range(2)]
-    plane = 4 * c + part
+    four = pl.ds(4 * c, 4)
     mine = pl.ds(pl.multiple_of(at.t * prow, prow), prow)
     probes = [
-        remote(probe_ref.at[plane], full_ref.at[plane, mine, :], ps.at[d], pr.at[d], at.s, at.tile_at(d))
+        remote(probe_ref.at[four], full_ref.at[four, mine, :], ps.at[d], pr.at[d], at.s, at.tile_at(d))
         for d in range(1, nt)
     ]
-    own_probe = pltpu.make_async_copy(probe_ref.at[plane], full_ref.at[plane, mine, :], loc_sem.at[0])
+    own_probe = pltpu.make_async_copy(probe_ref.at[four], full_ref.at[four, mine, :], loc_sem.at[0])
 
     def send(g):
         pl.when(jnp.logical_not(first))(strips[g].start)
@@ -116,9 +116,7 @@
     send(1)
     meanwhile()
 
-    half = n // 2
     cuts = [(0, step), (0, step), (0, step // 2), (step // 2, step // 2)]
-    spans = [pl.ds(0, n), pl.ds(0, n), pl.ds(0, half), pl.ds(half, half)]
     strip_z = [
         [
             remote(lower(g, *cuts[k]), lower(g, *cuts[k]), zs.at[g, k], zr.at[g, k], at.s_at_z(z + steps[k]), at.t)
@@ -126,32 +124,23 @@
         ]
         for g in range(2)
     ]
-    probe_z = [
-        remote(full_ref.at[plane, spans[k], :], full_ref.at[plane, spans[k], :], qs.at[k], qr.at[k],
-               at.s_at_z(z + steps[k]), at.t)
-        for k in range(4)
-    ]
     whole = [ext_ref.at[groups[g], pl.ds(height, height), :] for g in range(2)]
-    whole += [full_ref.at[pl.ds(4 * c, 4)]]
+    whole += [full_ref.at[four]]
     shares = [remote(whole[k], whole[k], cs.at[k], cr.at[k], at.s_core, at.t) for k in range(3)]
 
     arrived(0)
     for copy in strip_z[0]:
+        copy.start()
+    arrived(1)
+    for copy in strip_z[1]:
         copy.start()
     own_probe.wait()
     for copy in probes:
         copy.wait_recv()
-    for copy in probe_z:
-        copy.start()
+    shares[2].start()
     for copy in strip_z[0]:
         copy.wait_recv()
     shares[0].start()
-    arrived(1)
-    for copy in strip_z[1]:
-        copy.start()
-    for copy in probe_z:
-        copy.wait_recv()
-    shares[2].start()
     shares[0].wait_recv()
     shares[2].wait_recv()
 
@@ -166,7 +155,7 @@
     def drain():
         for strip in strips:
             pl.when(jnp.logical_not(first))(strip.wait_send)
-        for copy in probes + strip_z[0] + strip_z[1] + probe_z + shares:
+        for copy in probes + strip_z[0] + strip_z[1] + shares:
             copy.wait_send()
 
     return share_later, finish, drain
@@ -385,17 +374,15 @@
 
 
 STREAMS = ((0, 2), (2, 2), (4, 1))
-AHEAD = 2
 
 
 OWN = 7
 
 
 def sum_stage(at, nt, canvas, pgrad, gbuf, bufs, sems, drain):
-    got_c, got_p, pacc, first, upbuf, dnbuf, mine, pmine, ybuf, rimbuf, tbuf = bufs
-    cs, cr, us, ur, ds_, dr, ms, mr, ts, tr, gs, gr, ks, kr = sems
+    got_c, got_p, pacc, first, chain, mine, pmine, ybuf, rimbuf, tbuf = bufs
+    cs, cr, us, ur, ms, mr, ts, tr, gs, gr, ks, kr = sems
     nz = at.nz
-    half = nz // 2
     core, z = at.core, at.z
     own2 = pl.ds(2 * core, 2)
     other2 = pl.ds(2 - 2 * core, 2)
@@ -403,10 +390,7 @@
     def chunk(i):
         return lax.rem(i + 2 * nz, nz)
 
-    order = [half]
-    for k in range(half - 1, 0, -1):
-        order += [-k, k]
-    order += [0]
+    order = [8, -7, 4, -4, 7, -6, 3, -3, 6, -5, 2, -2, 5, 1, -1, 0]
 
     def swap_at(k):
         i = order.index(k)
@@ -414,8 +398,7 @@
 
     swap_p = remote(pgrad.at[other2], got_p, cs.at[nz], cr.at[nz], at.s_core, at.t)
     swaps = [swap_at(k) for k in order]
-    early = 2 + 2 * AHEAD
-    for copy in swaps[:2] + [swap_p] + swaps[2:early]:
+    for copy in swaps[:4] + [swap_p] + swaps[4:8]:
         copy.start()
 
     def probe_rows():
@@ -435,50 +418,52 @@
             return pacc[j]
         return canvas[2 * core + idx % 2, idx // 2, j] + got_c[idx % 2, idx // 2, j]
 
-    def up(i, p):
+    chains = [(8, 1, 4, True), (-7, -1, 3, True), (4, 1, 4, False), (-4, -1, 4, False)]
+    count = len(STREAMS)
+
+    def target(q, i):
+        return chains[q][0] - i * chains[q][1]
+
+    def hop(q, i, p):
+        _, way, hops, jumps = chains[q]
         part = pl.ds(*STREAMS[p])
-        src = first.at[0, part] if i == 0 else upbuf.at[i - 1, part]
-        return remote(src, upbuf.at[i, part], us.at[i, p], ur.at[i, p], at.s_at_z(z + 1), at.t)
-
-    def down(i, p):
-        part = pl.ds(*STREAMS[p])
-        src = first.at[1, part] if i == 0 else dnbuf.at[i - 1, part]
-        return remote(src, dnbuf.at[i, part], ds_.at[i, p], dr.at[i, p], at.s_at_z(z - 1), at.t)
-
-    count = len(STREAMS)
-    for k, r, start in ((half, 0, up), (1 - half, 1, down)):
-        swap_at(k).wait_recv()
+        src = first.at[q, part] if i == 0 else chain.at[q, i - 1, part]
+        to = target(q, i) if jumps and i == hops - 1 else way
+        return remote(src, chain.at[q, i, part], us.at[q, i, p], ur.at[q, i, p], at.s_at_z(z + to), at.t)
+
+    def span(p):
+        return range(STREAMS[p][0], STREAMS[p][0] + STREAMS[p][1])
+
+    for q in range(4):
+        swap_at(target(q, 0)).wait_recv()
         for p in range(count - 1):
-            for idx in range(STREAMS[p][0], STREAMS[p][0] + STREAMS[p][1]):
-                first[r, idx] = local(k, idx)
-            start(0, p).start()
+            for idx in span(p):
+                first[q, idx] = local(target(q, 0), idx)
+            hop(q, 0, p).start()
     probe_rows()
-    for k, r, start in ((half, 0, up), (1 - half, 1, down)):
-        first[r, 4] = local(k, 4)
-        start(0, count - 1).start()
-    for i in range(half):
-        ku, kd = half - 1 - i, 2 + i - half
-        for copy in swaps[early + 2 * i:early + 2 * i + 2]:
+    for q in range(4):
+        first[q, 4] = local(target(q, 0), 4)
+        hop(q, 0, count - 1).start()
+    for i in range(4):
+        for copy in swaps[8 + 4 * i:12 + 4 * i]:
             copy.start()
-        if i < half - 1:
-            swap_at(ku).wait_recv()
-        if i < half - 2:
-            swap_at(kd).wait_recv()
+        for q in range(4):
+            if i + 1 < chains[q][2]:
+                swap_at(target(q, i + 1)).wait_recv()
         for p in range(count):
-            span = range(STREAMS[p][0], STREAMS[p][0] + STREAMS[p][1])
-            up(i, p).wait_recv()
-            if i < half - 1:
-                for idx in span:
-                    upbuf[i, idx] += local(ku, idx)
-                up(i + 1, p).start()
-                down(i, p).wait_recv()
-            if i < half - 2:
-                for idx in span:
-                    dnbuf[i, idx] += local(kd, idx)
-                down(i + 1, p).start()
+            for q in range(4):
+                if i < chains[q][2]:
+                    hop(q, i, p).wait_recv()
+                if i + 1 < chains[q][2]:
+                    for idx in span(p):
+                        chain[q, i, idx] += local(target(q, i + 1), idx)
+                    hop(q, i + 1, p).start()
     swap_at(0).wait_recv()
     for idx in range(5):
-        mine[idx] = local(0, idx) + upbuf[half - 1, idx] + dnbuf[half - 2, idx]
+        total = local(0, idx)
+        for q in range(4):
+            total = total + chain[q, chains[q][2] - 1, idx]
+        mine[idx] = total
     for q in range(nt // 2):
         pmine[q] = mine[4, :, lanes * q:lanes * (q + 1)]
 
@@ -532,11 +517,10 @@
     drain()
     for copy in [swap_p, to_y, rim_a, rim_b] + swaps + tiles:
         copy.wait_send()
-    for p in range(count):
-        for i in range(half):
-            up(i, p).wait_send()
-        for i in range(half - 1):
-            down(i, p).wait_send()
+    for q in range(4):
+        for i in range(chains[q][2]):
+            for p in range(count):
+                hop(q, i, p).wait_send()
     near[3].wait_recv()
     near[2].wait_recv()
     near[1].wait_recv()
@@ -565,7 +549,7 @@
 
 def fused_kernel(ns, nt, off, spec, probe, meas_hbm, right_hbm, left_hbm, kern_hbm, gbuf, *scratch):
     ext, full, meas, right, left, kern, canvas, pgrad, xa, xb, ya, yb, patch, wave = scratch[:14]
-    selecting, bufs, sems = scratch[14:20], scratch[20:31], scratch[31:]
+    selecting, bufs, sems = scratch[14:20], scratch[20:30], scratch[30:]
     loads = [
         pltpu.make_async_copy(src, dst, sems[0].at[k])
         for k, (src, dst) in enumerate([(meas_hbm, meas), (right_hbm, right), (left_hbm, left), (kern_hbm, kern)])
@@ -576,18 +560,18 @@
     z = at.z
     greet(
         [(s, at.tile_at(d)) for s in (at.s, at.s_y) for d in range(1, nt)]
-        + [(at.s_at_z(z + d), at.t) for d in (1, -1, 2, -2, 6, -6)] + [(at.s_y, at.t), (at.s_core, at.t)]
+        + [(at.s_at_z(z + d), at.t) for d in (1, -1, 2, -2, 5, -5, 6, -6)] + [(at.s_y, at.t), (at.s_core, at.t)]
     )
 
     def split_own():
         split_rows(spec, selecting[0], 0, spec.shape[1], range(spec.shape[0]))
 
-    share_later, finish, drain = gather_stage(at, nt, spec, probe, ext, full, sems[1:12], split_own)
+    share_later, finish, drain = gather_stage(at, nt, spec, probe, ext, full, sems[1:10], split_own)
     for copy in loads:
         copy.wait()
     window_stage(at.t, off, ext, full, meas, right, left, kern, canvas, pgrad, xa, xb, ya, yb, patch, wave, *selecting,
                  share_later, finish)
-    sum_stage(at, nt, canvas, pgrad, gbuf, bufs, sems[12:], drain)
+    sum_stage(at, nt, canvas, pgrad, gbuf, bufs, sems[10:], drain)
 
 
 def place_kernel(ns, nt, gbuf, out, pout):
@@ -609,7 +593,6 @@
     modes, _, prow, n = probe_modes.shape
     planes = slices * two
     nz = ns // 4
-    half = nz // 2
     sub = height // nz
     count = len(STREAMS)
     right, left, kernel = dft_tables(n)
@@ -653,9 +636,8 @@
             f32(2, 2, nz, sub, width),
             f32(2, two, n, n),
             f32(nz, sub, width),
-            f32(2, 5, sub, width),
-            f32(half, 5, sub, width),
-            f32(half - 1, 5, sub, width),
+            f32(4, 5, sub, width),
+            f32(4, 4, 5, sub, width),
             f32(5, sub, width),
             f32(nt // 2, 8, n),
             f32(2, sub, width),
@@ -663,8 +645,8 @@
             f32(2, nt, 8, n),
         ]
         + [dma((4,))]
-        + [dma((3,))] + pair(2) + pair(nt) + pair(2, 4) + pair(4) + pair(3)
-        + pair(nz + 1) + pair(half, count) + pair(half - 1, count) + pair(3) + pair(2, nt) + pair(16) + pair(5),
+        + [dma((3,))] + pair(2) + pair(nt) + pair(2, 4) + pair(3)
+        + pair(nz + 1) + pair(4, 4, count) + pair(3) + pair(2, nt) + pair(16) + pair(5),
         compiler_params=pltpu.CompilerParams(collective_id=0, has_side_effects=True, vmem_limit_bytes=VMEM_LIMIT),
     )(
         offsets, specimen.reshape(planes, height, width), probe_modes.reshape(modes * two, prow, n), intensity,

time: 100 us -> 98 us (0.980)
  Pallas kernels: 99.4 us -> 97.2 us
    pallas_call x1, Pallas kernels: 97.1 us -> 94.9 us  [shards(): pl.pallas_call(partial(fused_kernel, ns, nt), name='gradient_sums', out_s...]
where the time goes in v3:
time: 98 us; the launch traced here: 97.8 us
  Pallas kernels  97.2 us (99%)
    pallas_call x1, Pallas kernels, shards(): pl.pallas_call(partial(fused_kernel, ns, nt), name='gradient_sums', out_s...  94.9 us
    pallas_call x1, Pallas kernels, shards(): pl.pallas_call(partial(place_kernel, ns, nt), name='place_rows', out_shap...  2.32 us

profile of v3, /device:TPU:1, one launch (start us, length us, event | category | flops | bytes accessed | tf_op | source)
XLA Modules:
  0.0 97.8 jit_solution(16401654628549415198)
XLA Ops:
  0.6 94.9 %gradient_sums.1.gbuf = f32[2,16,9,8,128]{4,3,2,1,0:T(8,128)} custom-call(s32[2,8]{1,0:T(2,128)} %off.1, f32[4,128,512]{2,1,0:T(8,128)} %bitcast.3, f32[8,16,128]{2,1,0:T(8,128)} %bitcast.4, f32[8,128,128]{2,1,0:T(8,128)} %meas_hbm.1, bf16[2,768,256]{2,1,0:T(8,128)(2,1)} %constant.6.clone.right_hbm, bf16[2,256,768]{2,1,0:T(8,128)(2,1)} %constant.7.clone.left_hbm, ...), custom_call_target="tpu_custom_call" | custom-call | tf_op jit(solution)/shard_map/gradient_sums/pallas_call | solution.py:609
  95.5 2.3 %place_rows.1 = (f32[4,16,8,512]{3,2,1,0:T(8,128)}, f32[4,2,16,128]{3,2,1,0:T(8,128)}) custom-call(f32[2,16,9,8,128]{4,3,2,1,0:T(8,128)} %gradient_sums.1.gbuf), custom_call_target="tpu_custom_call" | custom-call | tf_op jit(solution)/shard_map/place_rows/pallas_call | solution.py:655

commit v4 on v3

--- a/solution.py
+++ b/solution.py
@@ -191,14 +191,35 @@
     return jnp.where(condition, 1.0, 0.0).astype(BF16)
 
 
-def window_stage(owner, off_ref, ext_ref, probe_ref, meas_ref, right_ref, left_ref, kern_ref,
-                 canvas_ref, pgrad_ref, xa, xb, ya, yb, patch, wave, parts, cut, got, grads, tall, spread,
-                 share_later, finish):
+def slots_of(off_ref, owner, height):
+    per_group = off_ref.shape[1]
+    far = 8 * height
+    hits, corners = [], []
+    for slot in range(CAP):
+        rank = jnp.int32(0)
+        row = jnp.int32(far)
+        col = jnp.int32(0)
+        chosen = []
+        for b in range(per_group):
+            here = ((off_ref[0, b] // height) == owner).astype(jnp.int32)
+            hit = here * (rank == slot).astype(jnp.int32)
+            row = row + hit * (off_ref[0, b] - owner * height - far)
+            col = col + hit * off_ref[1, b]
+            chosen.append(hit.astype(F32))
+            rank = rank + here
+        hits.append(chosen)
+        corners.append((row, col))
+    return hits, corners
+
+
+def window_stage(at, slots, per_group, ext_ref, probe_ref, meas_ref, right_ref, left_ref, kern_ref,
+                 canvas_ref, pgrad_ref, xa, xb, ya, yb, patch, wave, parts, cut, got, wgrad, got_w, tall, spread, put_got,
+                 share_later, finish, swap_w, swap_p, swap_put):
     planes, height2, width = ext_ref.shape
     height = height2 // 2
     n = probe_ref.shape[1]
     modes = probe_ref.shape[0] // 2
-    per_group = off_ref.shape[1]
+    hits, corners = slots
     batch = [(slot, m) for slot in range(CAP) for m in range(modes)]
 
     def dot(a, b):
@@ -239,22 +260,6 @@
             re, im = left_parts(out, b)
             put_left(dst, b, n, 0, re * kre - im * kim)
             put_left(dst, b, n, 1, re * kim + im * kre)
-
-    hits, corners = [], []
-    for slot in range(CAP):
-        rank = jnp.int32(0)
-        row = jnp.int32(4 * height2)
-        col = jnp.int32(0)
-        chosen = []
-        for b in range(per_group):
-            here = ((off_ref[0, b] // height) == owner).astype(jnp.int32)
-            hit = here * (rank == slot).astype(jnp.int32)
-            row = row + hit * (off_ref[0, b] - owner * height - 4 * height2)
-            col = col + hit * off_ref[1, b]
-            chosen.append(hit.astype(F32))
-            rank = rank + here
-        hits.append(chosen)
-        corners.append((row, col))
 
     def iotas(*shape):
         return [lax.broadcasted_iota(jnp.int32, shape, axis) for axis in range(2)]
@@ -317,11 +322,6 @@
     left_to_right(yb, xb, 1)
     out = mul_right(xb, 1)
 
-    def pad_window(slot, p, grad):
-        high = grad.astype(BF16)
-        grads[slot, :, pl.ds(2 * p * n, n)] = high
-        grads[slot, :, pl.ds((2 * p + 1) * n, n)] = (grad - high.astype(F32)).astype(BF16)
-
     for slot in range(CAP):
         gre = jnp.zeros((n, n), F32)
         gim = jnp.zeros((n, n), F32)
@@ -333,8 +333,8 @@
             gim = gim + wre * im - wim * re
             put_right(xa, b, n, 0, patch[slot, 2] * re + patch[slot, 3] * im)
             put_right(xa, b, n, 1, patch[slot, 2] * im - patch[slot, 3] * re)
-        pad_window(slot, 2, gre)
-        pad_window(slot, 3, gim)
+        wgrad[slot, 2] = gre
+        wgrad[slot, 3] = gim
     right_to_left(xa, ya, 0)
     through_kernel(ya, yb, -1.0)
     left_to_right(yb, xb, 1)
@@ -348,6 +348,7 @@
             pgim = pgim + patch[slot, 0] * im - patch[slot, 1] * re
         pgrad_ref[m, 0] = pgre
         pgrad_ref[m, 1] = pgim
+    swap_p.start()
     for slot in range(CAP):
         hre = jnp.zeros((n, n), F32)
         him = jnp.zeros((n, n), F32)
@@ -356,20 +357,34 @@
             pre, pim = probe_ref[2 * m], probe_ref[2 * m + 1]
             hre = hre + pre * re + pim * im
             him = him + pre * im - pim * re
-        pad_window(slot, 0, hre)
-        pad_window(slot, 1, him)
-
+        wgrad[slot, 0] = hre
+        wgrad[slot, 1] = him
+
+    swap_w.start()
     i, j = iotas(height2, n)
     u, v = iotas(n, width)
+
+    def put(e, row, col, windows):
+        pieces = []
+        for value in windows:
+            high = value.astype(BF16)
+            pieces += [high, (value - high.astype(F32)).astype(BF16)]
+        out = dot(select(i == j + row), jnp.concatenate(pieces, 1))
+        columns = select(v == u + col)
+        for part in range(2):
+            lanes = pl.ds((2 * e + part) * n, n)
+            for q in range(2):
+                piece = out[:, (2 * q + part) * n:(2 * q + part + 1) * n]
+                tall[pl.ds(q * height2, height2), lanes] = piece.astype(BF16)
+            spread[pl.ds((2 * e + part) * n, n), :] = columns
+
     for slot, (row, col) in enumerate(corners):
-        out = dot(select(i == j + row), grads[slot])
-        for p in range(planes):
-            for part in range(2):
-                piece = out[:, (2 * p + part) * n:(2 * p + part + 1) * n]
-                tall[pl.ds(p * height2, height2), pl.ds((2 * slot + part) * n, n)] = piece.astype(BF16)
-        put = select(v == u + col)
-        spread[pl.ds(2 * slot * n, n), :] = put
-        spread[pl.ds((2 * slot + 1) * n, n), :] = put
+        put(slot, row, col, [wgrad[slot, 2 * at.core + q] for q in range(2)])
+    swap_put.wait_recv()
+    swap_w.wait_recv()
+    for slot in range(CAP):
+        row, col = put_got[2 * slot:2 * slot + 1, :n], put_got[2 * slot + 1:2 * slot + 2, :]
+        put(CAP + slot, row, col, [got_w[slot, q] for q in range(2)])
     canvas_ref[...] = dot(tall[...], spread[...]).reshape(canvas_ref.shape)
 
 
@@ -379,27 +394,15 @@
 OWN = 7
 
 
-def sum_stage(at, nt, canvas, pgrad, gbuf, bufs, sems, drain):
-    got_c, got_p, pacc, first, chain, mine, pmine, ybuf, rimbuf, tbuf = bufs
-    cs, cr, us, ur, ms, mr, ts, tr, gs, gr, ks, kr = sems
+def sum_stage(at, nt, canvas, pgrad, gbuf, bufs, sems, swap_p, drain):
+    got_p, pacc, chain, mine, pmine, ybuf, rimbuf, tbuf = bufs
+    us, ur, ms, mr, ts, tr, gs, gr, ks, kr = sems
     nz = at.nz
     core, z = at.core, at.z
-    own2 = pl.ds(2 * core, 2)
-    other2 = pl.ds(2 - 2 * core, 2)
     lanes = 128
+
     def chunk(i):
         return lax.rem(i + 2 * nz, nz)
-
-    order = [8, -7, 4, -4, 7, -6, 3, -3, 6, -5, 2, -2, 5, 1, -1, 0]
-
-    def swap_at(k):
-        i = order.index(k)
-        return remote(canvas.at[other2, :, chunk(z + k)], got_c.at[:, :, chunk(z + k)], cs.at[i], cr.at[i], at.s_core, at.t)
-
-    swap_p = remote(pgrad.at[other2], got_p, cs.at[nz], cr.at[nz], at.s_core, at.t)
-    swaps = [swap_at(k) for k in order]
-    for copy in swaps[:4] + [swap_p] + swaps[4:8]:
-        copy.start()
 
     def probe_rows():
         swap_p.wait_recv()
@@ -410,13 +413,13 @@
                     j = (2 * m + ri) * 4 + r
                     for t in range(nt):
                         piece = whole[16 * t + 4 * r:16 * t + 4 * r + 4]
-                        pacc[j, pl.ds(4 * (t % 2), 4), pl.ds(lanes * (t // 2), lanes)] = piece
+                        pacc[j, 0, pl.ds(4 * (t % 2), 4), pl.ds(lanes * (t // 2), lanes)] = piece
 
     def local(k, idx):
-        j = chunk(z + k)
-        if idx == 4:
-            return pacc[j]
-        return canvas[2 * core + idx % 2, idx // 2, j] + got_c[idx % 2, idx // 2, j]
+        return pacc[chunk(z + k), 0] if idx == 4 else canvas[idx % 2, idx // 2, chunk(z + k)]
+
+    def local_part(k, p):
+        return pacc.at[chunk(z + k)] if p == 2 else canvas.at[:, p, chunk(z + k)]
 
     chains = [(8, 1, 4, True), (-7, -1, 3, True), (4, 1, 4, False), (-4, -1, 4, False)]
     count = len(STREAMS)
@@ -427,29 +430,20 @@
     def hop(q, i, p):
         _, way, hops, jumps = chains[q]
         part = pl.ds(*STREAMS[p])
-        src = first.at[q, part] if i == 0 else chain.at[q, i - 1, part]
+        src = local_part(target(q, 0), p) if i == 0 else chain.at[q, i - 1, part]
         to = target(q, i) if jumps and i == hops - 1 else way
         return remote(src, chain.at[q, i, part], us.at[q, i, p], ur.at[q, i, p], at.s_at_z(z + to), at.t)
 
     def span(p):
         return range(STREAMS[p][0], STREAMS[p][0] + STREAMS[p][1])
 
-    for q in range(4):
-        swap_at(target(q, 0)).wait_recv()
-        for p in range(count - 1):
-            for idx in span(p):
-                first[q, idx] = local(target(q, 0), idx)
+    for p in range(count - 1):
+        for q in range(4):
             hop(q, 0, p).start()
     probe_rows()
     for q in range(4):
-        first[q, 4] = local(target(q, 0), 4)
         hop(q, 0, count - 1).start()
     for i in range(4):
-        for copy in swaps[8 + 4 * i:12 + 4 * i]:
-            copy.start()
-        for q in range(4):
-            if i + 1 < chains[q][2]:
-                swap_at(target(q, i + 1)).wait_recv()
         for p in range(count):
             for q in range(4):
                 if i < chains[q][2]:
@@ -458,7 +452,6 @@
                     for idx in span(p):
                         chain[q, i, idx] += local(target(q, i + 1), idx)
                     hop(q, i + 1, p).start()
-    swap_at(0).wait_recv()
     for idx in range(5):
         total = local(0, idx)
         for q in range(4):
@@ -515,7 +508,7 @@
     for copy in far + near:
         copy.start()
     drain()
-    for copy in [swap_p, to_y, rim_a, rim_b] + swaps + tiles:
+    for copy in [to_y, rim_a, rim_b] + tiles:
         copy.wait_send()
     for q in range(4):
         for i in range(chains[q][2]):
@@ -549,7 +542,7 @@
 
 def fused_kernel(ns, nt, off, spec, probe, meas_hbm, right_hbm, left_hbm, kern_hbm, gbuf, *scratch):
     ext, full, meas, right, left, kern, canvas, pgrad, xa, xb, ya, yb, patch, wave = scratch[:14]
-    selecting, bufs, sems = scratch[14:20], scratch[20:30], scratch[30:]
+    selecting, put_own, bufs, sems = scratch[14:22], scratch[22], scratch[23:31], scratch[31:]
     loads = [
         pltpu.make_async_copy(src, dst, sems[0].at[k])
         for k, (src, dst) in enumerate([(meas_hbm, meas), (right_hbm, right), (left_hbm, left), (kern_hbm, kern)])
@@ -563,15 +556,35 @@
         + [(at.s_at_z(z + d), at.t) for d in (1, -1, 2, -2, 5, -5, 6, -6)] + [(at.s_y, at.t), (at.s_core, at.t)]
     )
 
+    slots = slots_of(off, at.t, spec.shape[1])
+    corners = sum(slots[1], ())
+    lines = lax.broadcasted_iota(jnp.int32, put_own.shape, 0)
+    places = jnp.zeros(put_own.shape, jnp.int32)
+    for k, value in enumerate(corners):
+        places = jnp.where(lines == k, value, places)
+    put_own[...] = places
+    wgrad, got_w, put_got = selecting[3], selecting[4], selecting[7]
+    cs, cr = sems[10:12]
+    swap_put = remote(put_own, put_got, cs.at[0], cr.at[0], at.s_core, at.t)
+    swap_w = remote(wgrad.at[:, pl.ds(2 - 2 * at.core, 2)], got_w, cs.at[1], cr.at[1], at.s_core, at.t)
+    swap_p = remote(pgrad.at[pl.ds(2 - 2 * at.core, 2)], bufs[0], cs.at[2], cr.at[2], at.s_core, at.t)
+
     def split_own():
+        swap_put.start()
         split_rows(spec, selecting[0], 0, spec.shape[1], range(spec.shape[0]))
 
     share_later, finish, drain = gather_stage(at, nt, spec, probe, ext, full, sems[1:10], split_own)
     for copy in loads:
         copy.wait()
-    window_stage(at.t, off, ext, full, meas, right, left, kern, canvas, pgrad, xa, xb, ya, yb, patch, wave, *selecting,
-                 share_later, finish)
-    sum_stage(at, nt, canvas, pgrad, gbuf, bufs, sems[10:], drain)
+    window_stage(at, slots, off.shape[1], ext, full, meas, right, left, kern, canvas, pgrad, xa, xb, ya, yb, patch, wave, *selecting,
+                 share_later, finish, swap_w, swap_p, swap_put)
+
+    def drain_all():
+        drain()
+        for copy in (swap_put, swap_w, swap_p):
+            copy.wait_send()
+
+    sum_stage(at, nt, canvas, pgrad, gbuf, bufs, sems[12:], swap_p, drain_all)
 
 
 def place_kernel(ns, nt, gbuf, out, pout):
@@ -619,7 +632,7 @@
             pltpu.VMEM(right.shape, BF16),
             pltpu.VMEM(left.shape, BF16),
             f32(2, n, n),
-            f32(planes, 2, nz, sub, width),
+            f32(2, 2, nz, sub, width),
             f32(modes, two, n, n),
             pltpu.VMEM((CAP * modes * n, 6 * n), BF16),
             pltpu.VMEM((CAP * modes * n, 6 * n), BF16),
@@ -630,13 +643,14 @@
             pltpu.VMEM((2 * planes, 2 * height, width), BF16),
             pltpu.VMEM((width, CAP * n), BF16),
             pltpu.VMEM((CAP, 4 * height, planes * n), BF16),
-            pltpu.VMEM((CAP, n, 2 * planes * n), BF16),
-            pltpu.VMEM((planes * 2 * height, 2 * CAP * n), BF16),
-            pltpu.VMEM((2 * CAP * n, width), BF16),
-            f32(2, 2, nz, sub, width),
+            f32(CAP, planes, n, n),
+            f32(CAP, 2, n, n),
+            pltpu.VMEM((4 * height, 4 * CAP * n), BF16),
+            pltpu.VMEM((4 * CAP * n, width), BF16),
+            pltpu.VMEM((8, width), jnp.int32),
+            pltpu.VMEM((8, width), jnp.int32),
             f32(2, two, n, n),
-            f32(nz, sub, width),
-            f32(4, 5, sub, width),
+            f32(nz, 1, sub, width),
             f32(4, 4, 5, sub, width),
             f32(5, sub, width),
             f32(nt // 2, 8, n),
@@ -646,7 +660,7 @@
         ]
         + [dma((4,))]
         + [dma((3,))] + pair(2) + pair(nt) + pair(2, 4) + pair(3)
-        + pair(nz + 1) + pair(4, 4, count) + pair(3) + pair(2, nt) + pair(16) + pair(5),
+        + pair(3) + pair(4, 4, count) + pair(3) + pair(2, nt) + pair(16) + pair(5),
         compiler_params=pltpu.CompilerParams(collective_id=0, has_side_effects=True, vmem_limit_bytes=VMEM_LIMIT),
     )(
         offsets, specimen.reshape(planes, height, width), probe_modes.reshape(modes * two, prow, n), intensity,

time: 98 us -> 97.5 us (level)
  no operation moved by 1% of the time
where the time goes in v4:
time: 97.5 us; the launch traced here: 97.3 us
  Pallas kernels  96.7 us (99%)
    pallas_call x1, Pallas kernels, shards(): pl.pallas_call(partial(fused_kernel, ns, nt), name='gradient_sums', out_s...  94.3 us
    pallas_call x1, Pallas kernels, shards(): pl.pallas_call(partial(place_kernel, ns, nt), name='place_rows', out_shap...  2.32 us

profile of v4, /device:TPU:1, one launch (start us, length us, event | category | flops | bytes accessed | tf_op | source)
XLA Modules:
  0.0 97.3 jit_solution(15043259957379600633)
XLA Ops:
  0.6 94.3 %gradient_sums.1.gbuf = f32[2,16,9,8,128]{4,3,2,1,0:T(8,128)} custom-call(s32[2,8]{1,0:T(2,128)} %off.1, f32[4,128,512]{2,1,0:T(8,128)} %bitcast.3, f32[8,16,128]{2,1,0:T(8,128)} %bitcast.4, f32[8,128,128]{2,1,0:T(8,128)} %meas_hbm.1, bf16[2,768,256]{2,1,0:T(8,128)(2,1)} %constant.6.clone.right_hbm, bf16[2,256,768]{2,1,0:T(8,128)(2,1)} %constant.7.clone.left_hbm, ...), custom_call_target="tpu_custom_call" | custom-call | tf_op jit(solution)/shard_map/gradient_sums/pallas_call | solution.py:622
  95.0 2.3 %place_rows.1 = (f32[4,16,8,512]{3,2,1,0:T(8,128)}, f32[4,2,16,128]{3,2,1,0:T(8,128)}) custom-call(f32[2,16,9,8,128]{4,3,2,1,0:T(8,128)} %gradient_sums.1.gbuf), custom_call_target="tpu_custom_call" | custom-call | tf_op jit(solution)/shard_map/place_rows/pallas_call | solution.py:669

commit v5 on v4

--- a/solution.py
+++ b/solution.py
@@ -388,15 +388,15 @@
     canvas_ref[...] = dot(tall[...], spread[...]).reshape(canvas_ref.shape)
 
 
-STREAMS = ((0, 2), (2, 2), (4, 1))
+STREAMS = ((0, 2), (2, 2))
 
 
 OWN = 7
 
 
 def sum_stage(at, nt, canvas, pgrad, gbuf, bufs, sems, swap_p, drain):
-    got_p, pacc, chain, mine, pmine, ybuf, rimbuf, tbuf = bufs
-    us, ur, ms, mr, ts, tr, gs, gr, ks, kr = sems
+    got_p, psum, tbuf, zsend, zbuf, pmine, pybuf, chain, mine, ybuf, rimbuf = bufs
+    us, ur, ms, mr, ts, tr, zs, zr, gs, gr, ks, kr = sems
     nz = at.nz
     core, z = at.core, at.z
     lanes = 128
@@ -404,22 +404,51 @@
     def chunk(i):
         return lax.rem(i + 2 * nz, nz)
 
-    def probe_rows():
+    pz = zsend.shape[0]
+    prow = tbuf.shape[3]
+
+    def rows_of(t):
+        return pl.ds(pl.multiple_of(t * prow, prow), prow)
+
+    tiles = [
+        remote(psum.at[:, :, rows_of(at.tile_at(d)), :], tbuf.at[at.t], ts.at[d], tr.at[d], at.s, at.tile_at(d))
+        for d in range(1, nt)
+    ]
+    zcopies = [
+        remote(zsend.at[lax.rem(z + d, pz)], zbuf.at[z], zs.at[d], zr.at[d], at.s_at_z(z + d), at.t)
+        for d in range(1, nz)
+    ]
+    py = remote(pmine, pybuf, ms.at[3], mr.at[3], at.s_y, at.t)
+
+    def core_stage():
         swap_p.wait_recv()
-        for m in range(2):
-            for ri in range(2):
-                whole = pgrad[2 * core + m, ri] + got_p[m, ri]
-                for r in range(4):
-                    j = (2 * m + ri) * 4 + r
-                    for t in range(nt):
-                        piece = whole[16 * t + 4 * r:16 * t + 4 * r + 4]
-                        pacc[j, 0, pl.ds(4 * (t % 2), 4), pl.ds(lanes * (t // 2), lanes)] = piece
+        psum[...] = pgrad[pl.ds(2 * core, 2)] + got_p[...]
+        for copy in tiles:
+            copy.start()
+        tbuf[at.t] = psum[:, :, rows_of(at.t), :]
+
+    def tile_stage():
+        for copy in tiles:
+            copy.wait_recv()
+        total = tbuf[0]
+        for t in range(1, nt):
+            total = total + tbuf[t]
+        zsend[...] = total.reshape(zsend.shape)
+        for copy in zcopies:
+            copy.start()
+        zbuf[z] = zsend[lax.rem(z, pz)]
+
+    def z_stage():
+        for copy in zcopies:
+            copy.wait_recv()
+        total = zbuf[0]
+        for j in range(1, nz):
+            total = total + zbuf[j]
+        pmine[...] = total
+        py.start()
 
     def local(k, idx):
-        return pacc[chunk(z + k), 0] if idx == 4 else canvas[idx % 2, idx // 2, chunk(z + k)]
-
-    def local_part(k, p):
-        return pacc.at[chunk(z + k)] if p == 2 else canvas.at[:, p, chunk(z + k)]
+        return canvas[idx % 2, idx // 2, chunk(z + k)]
 
     chains = [(8, 1, 4, True), (-7, -1, 3, True), (4, 1, 4, False), (-4, -1, 4, False)]
     count = len(STREAMS)
@@ -430,19 +459,17 @@
     def hop(q, i, p):
         _, way, hops, jumps = chains[q]
         part = pl.ds(*STREAMS[p])
-        src = local_part(target(q, 0), p) if i == 0 else chain.at[q, i - 1, part]
+        src = canvas.at[:, p, chunk(z + target(q, 0))] if i == 0 else chain.at[q, i - 1, part]
         to = target(q, i) if jumps and i == hops - 1 else way
         return remote(src, chain.at[q, i, part], us.at[q, i, p], ur.at[q, i, p], at.s_at_z(z + to), at.t)
 
     def span(p):
         return range(STREAMS[p][0], STREAMS[p][0] + STREAMS[p][1])
 
-    for p in range(count - 1):
+    for p in range(count):
         for q in range(4):
             hop(q, 0, p).start()
-    probe_rows()
-    for q in range(4):
-        hop(q, 0, count - 1).start()
+    core_stage()
     for i in range(4):
         for p in range(count):
             for q in range(4):
@@ -452,27 +479,24 @@
                     for idx in span(p):
                         chain[q, i, idx] += local(target(q, i + 1), idx)
                     hop(q, i + 1, p).start()
-    for idx in range(5):
+        if i == 1:
+            tile_stage()
+        if i == 2:
+            z_stage()
+    for idx in range(4):
         total = local(0, idx)
         for q in range(4):
             total = total + chain[q, chains[q][2] - 1, idx]
         mine[idx] = total
-    for q in range(nt // 2):
-        pmine[q] = mine[4, :, lanes * q:lanes * (q + 1)]
 
     to_y = remote(mine.at[pl.ds(0, 2)], ybuf, ms.at[0], mr.at[0], at.s_y, at.t)
     rim_a = remote(mine.at[pl.ds(2, 2)], rimbuf.at[0], ms.at[1], mr.at[1], at.s, at.tile_at(1))
     rim_b = remote(mine.at[pl.ds(2, 2)], rimbuf.at[1], ms.at[2], mr.at[2], at.s_y, at.tile_at(1))
-    tiles = [
-        remote(pmine.at[at.tile_at(d) // 2], tbuf.at[at.ylo, at.t], ts.at[e, d], tr.at[e, d], s, at.tile_at(d))
-        for e, s in ((0, at.s), (1, at.s_y)) for d in range(e ^ 1, nt)
-    ]
     rim_b.start()
     rim_a.start()
     to_y.start()
-    for copy in tiles:
-        copy.start()
-    tbuf[at.ylo, at.t] = pmine[at.t // 2]
+    py.wait_recv()
+    gbuf[core, OWN, 8] = pmine[...] + pybuf[...]
     to_y.wait_recv()
     rim_a.wait_recv()
     rim_b.wait_recv()
@@ -480,12 +504,6 @@
         final = (mine[k] + ybuf[k]) + (rimbuf[0, k] + rimbuf[1, k])
         for l in range(4):
             gbuf[core, OWN, 4 * k + l] = final[:, lanes * l:lanes * (l + 1)]
-    for copy in tiles:
-        copy.wait_recv()
-    total = tbuf[0, 0]
-    for k in range(1, 2 * nt):
-        total = total + tbuf[k // nt, k % nt]
-    gbuf[core, OWN, 8] = jnp.where(lax.rem(at.t, 2) == 1, pltpu.roll(total, 4, 0), total)
 
     def pass_on(i, k, to, part=slice(0, 9)):
         new = k - to + 16 * (k - to < -OWN)
@@ -508,7 +526,7 @@
     for copy in far + near:
         copy.start()
     drain()
-    for copy in [to_y, rim_a, rim_b] + tiles:
+    for copy in [to_y, rim_a, rim_b, py] + tiles + zcopies:
         copy.wait_send()
     for q in range(4):
         for i in range(chains[q][2]):
@@ -542,7 +560,7 @@
 
 def fused_kernel(ns, nt, off, spec, probe, meas_hbm, right_hbm, left_hbm, kern_hbm, gbuf, *scratch):
     ext, full, meas, right, left, kern, canvas, pgrad, xa, xb, ya, yb, patch, wave = scratch[:14]
-    selecting, put_own, bufs, sems = scratch[14:22], scratch[22], scratch[23:31], scratch[31:]
+    selecting, put_own, bufs, sems = scratch[14:22], scratch[22], scratch[23:34], scratch[34:]
     loads = [
         pltpu.make_async_copy(src, dst, sems[0].at[k])
         for k, (src, dst) in enumerate([(meas_hbm, meas), (right_hbm, right), (left_hbm, left), (kern_hbm, kern)])
@@ -553,7 +571,7 @@
     z = at.z
     greet(
         [(s, at.tile_at(d)) for s in (at.s, at.s_y) for d in range(1, nt)]
-        + [(at.s_at_z(z + d), at.t) for d in (1, -1, 2, -2, 5, -5, 6, -6)] + [(at.s_y, at.t), (at.s_core, at.t)]
+        + [(at.s_at_z(z + d), at.t) for d in range(1, at.nz)] + [(at.s_y, at.t), (at.s_core, at.t)]
     )
 
     slots = slots_of(off, at.t, spec.shape[1])
@@ -597,8 +615,9 @@
             for k in range(2):
                 for l in range(4):
                     out[2 * c + k, j, :, lanes * l:lanes * (l + 1)] = gbuf[c, slot, 4 * k + l]
-            m, ri, r = j // 8, (j // 4) % 2, j % 4
-            pout[2 * c + m, ri, pl.ds(4 * r, 4), :] = gbuf[c, slot, 8, 0:4]
+            if j < nz // 2:
+                m, ri, h = j // 4, (j // 2) % 2, j % 2
+                pout[2 * c + m, ri, pl.ds(8 * h, 8), :] = gbuf[c, slot, 8]
 
 
 def shards(ns, nt, specimen, probe_modes, offsets, intensity):
@@ -650,17 +669,20 @@
             pltpu.VMEM((8, width), jnp.int32),
             pltpu.VMEM((8, width), jnp.int32),
             f32(2, two, n, n),
-            f32(nz, 1, sub, width),
-            f32(4, 4, 5, sub, width),
-            f32(5, sub, width),
-            f32(nt // 2, 8, n),
+            f32(2, two, n, n),
+            f32(nt, 2, two, prow, n),
+            f32(2 * two * prow // 8, 8, n),
+            f32(nz, 8, n),
+            f32(8, n),
+            f32(8, n),
+            f32(4, 4, 4, sub, width),
+            f32(4, sub, width),
             f32(2, sub, width),
             f32(2, 2, sub, width),
-            f32(2, nt, 8, n),
         ]
         + [dma((4,))]
         + [dma((3,))] + pair(2) + pair(nt) + pair(2, 4) + pair(3)
-        + pair(3) + pair(4, 4, count) + pair(3) + pair(2, nt) + pair(16) + pair(5),
+        + pair(3) + pair(4, 4, count) + pair(4) + pair(nt) + pair(nz) + pair(16) + pair(5),
         compiler_params=pltpu.CompilerParams(collective_id=0, has_side_effects=True, vmem_limit_bytes=VMEM_LIMIT),
     )(
         offsets, specimen.reshape(planes, height, width), probe_modes.reshape(modes * two, prow, n), intensity,

time: 97.5 us -> 94.2 us (0.966); the launches traced: 97.3 us -> 92.5 us
  Pallas kernels: 96.7 us -> 91.8 us
    pallas_call x1, Pallas kernels: 94.3 us -> 89.5 us  [shards(): pl.pallas_call(partial(fused_kernel, ns, nt), name='gradient_sums', out_s...]
where the time goes in v5:
time: 94.2 us; the launch traced here: 92.5 us
  Pallas kernels  91.8 us (97%)
    pallas_call x1, Pallas kernels, shards(): pl.pallas_call(partial(fused_kernel, ns, nt), name='gradient_sums', out_s...  89.5 us
    pallas_call x1, Pallas kernels, shards(): pl.pallas_call(partial(place_kernel, ns, nt), name='place_rows', out_shap...  2.34 us

profile of v5, /device:TPU:1, one launch (start us, length us, event | category | flops | bytes accessed | tf_op | source)
XLA Modules:
  0.0 92.5 jit_solution(18185401019190993562)
XLA Ops:
  0.6 89.5 %gradient_sums.1.gbuf = f32[2,16,9,8,128]{4,3,2,1,0:T(8,128)} custom-call(s32[2,8]{1,0:T(2,128)} %off.1, f32[4,128,512]{2,1,0:T(8,128)} %bitcast.3, f32[8,16,128]{2,1,0:T(8,128)} %bitcast.4, f32[8,128,128]{2,1,0:T(8,128)} %meas_hbm.1, bf16[2,768,256]{2,1,0:T(8,128)(2,1)} %constant.6.clone.right_hbm, bf16[2,256,768]{2,1,0:T(8,128)(2,1)} %constant.7.clone.left_hbm, ...), custom_call_target="tpu_custom_call" | custom-call | tf_op jit(solution)/shard_map/gradient_sums/pallas_call | solution.py:641
  90.1 2.3 %place_rows.1 = (f32[4,16,8,512]{3,2,1,0:T(8,128)}, f32[4,2,16,128]{3,2,1,0:T(8,128)}) custom-call(f32[2,16,9,8,128]{4,3,2,1,0:T(8,128)} %gradient_sums.1.gbuf), custom_call_target="tpu_custom_call" | custom-call | tf_op jit(solution)/shard_map/place_rows/pallas_call | solution.py:691

commit v6 on v5

--- a/solution.py
+++ b/solution.py
@@ -492,14 +492,19 @@
     to_y = remote(mine.at[pl.ds(0, 2)], ybuf, ms.at[0], mr.at[0], at.s_y, at.t)
     rim_a = remote(mine.at[pl.ds(2, 2)], rimbuf.at[0], ms.at[1], mr.at[1], at.s, at.tile_at(1))
     rim_b = remote(mine.at[pl.ds(2, 2)], rimbuf.at[1], ms.at[2], mr.at[2], at.s_y, at.tile_at(1))
-    rim_b.start()
-    rim_a.start()
+    for rim in (rim_b, rim_a):
+        pl.when(at.t < nt - 1)(rim.start)
     to_y.start()
+
+    @pl.when(at.t == 0)
+    def _():
+        rimbuf[...] = jnp.zeros_like(rimbuf)
+
     py.wait_recv()
     gbuf[core, OWN, 8] = pmine[...] + pybuf[...]
     to_y.wait_recv()
-    rim_a.wait_recv()
-    rim_b.wait_recv()
+    for rim in (rim_a, rim_b):
+        pl.when(at.t > 0)(rim.wait_recv)
     for k in range(2):
         final = (mine[k] + ybuf[k]) + (rimbuf[0, k] + rimbuf[1, k])
         for l in range(4):
@@ -526,7 +531,9 @@
     for copy in far + near:
         copy.start()
     drain()
-    for copy in [to_y, rim_a, rim_b, py] + tiles + zcopies:
+    for rim in (rim_a, rim_b):
+        pl.when(at.t < nt - 1)(rim.wait_send)
+    for copy in [to_y, py] + tiles + zcopies:
         copy.wait_send()
     for q in range(4):
         for i in range(chains[q][2]):

time: 94.2 us -> 94.2 us (level)
  the two profiles are of different devices: /device:TPU:1 before, /device:TPU:17 now
where the time goes in v6:
time: 94.2 us; the launch traced here: 94.1 us
  Pallas kernels  93.4 us (99%)
    pallas_call x1, Pallas kernels, shards(): pl.pallas_call(partial(fused_kernel, ns, nt), name='gradient_sums', out_s...  91.1 us
    pallas_call x1, Pallas kernels, shards(): pl.pallas_call(partial(place_kernel, ns, nt), name='place_rows', out_shap...  2.34 us

profile of v6, /device:TPU:17, one launch (start us, length us, event | category | flops | bytes accessed | tf_op | source)
XLA Modules:
  0.0 94.1 jit_solution(2634401297747059227)
XLA Ops:
  0.6 91.1 %gradient_sums.1.gbuf = f32[2,16,9,8,128]{4,3,2,1,0:T(8,128)} custom-call(s32[2,8]{1,0:T(2,128)} %off.1, f32[4,128,512]{2,1,0:T(8,128)} %bitcast.3, f32[8,16,128]{2,1,0:T(8,128)} %bitcast.4, f32[8,128,128]{2,1,0:T(8,128)} %meas_hbm.1, bf16[2,768,256]{2,1,0:T(8,128)(2,1)} %constant.6.clone.right_hbm, bf16[2,256,768]{2,1,0:T(8,128)(2,1)} %constant.7.clone.left_hbm, ...), custom_call_target="tpu_custom_call" | custom-call | tf_op jit(solution)/shard_map/gradient_sums/pallas_call | solution.py:648
  91.7 2.3 %place_rows.1 = (f32[4,16,8,512]{3,2,1,0:T(8,128)}, f32[4,2,16,128]{3,2,1,0:T(8,128)}) custom-call(f32[2,16,9,8,128]{4,3,2,1,0:T(8,128)} %gradient_sums.1.gbuf), custom_call_target="tpu_custom_call" | custom-call | tf_op jit(solution)/shard_map/place_rows/pallas_call | solution.py:698
